TPU v7x, 256 devices: a whole 4x4x8 slice. The times are simulated.
256 devices in a mesh: ctx: 16 (over y, x_hi, core), exp: 16 (over z, x_lo).
Axes of the slice: x: 4 (x_hi: 2, x_lo: 2; x = x_hi * 2 + x_lo), y: 4, z: 8, core: 2. Of those that a mesh axis runs over, the one named last changes fastest.
Arguments:
- queries: bfloat16 [32768, 16, 128], P(('ctx', 'exp')), may hold values from -6 to 6
- key_tensor: bfloat16 [32768, 2, 128], P(('ctx', 'exp')), may hold values from -6 to 6
- value_tensor: bfloat16 [32768, 2, 128], P(('ctx', 'exp')), may hold values from -6 to 6
- out_grad: bfloat16 [32768, 16, 128], P(('ctx', 'exp')), may hold values from -120 to 120
- log_norm: float32 [32768, 16], P(('ctx', 'exp')), may hold values from 6.5 to 8
- out_dot: float32 [32768, 16], P(('ctx', 'exp')), may hold values from -1200 to 1200
- span_order: int32 [32], replicated, may hold values from 0 to 31, each once
- moe_input: bfloat16 [32768, 2048], P(('ctx', 'exp')), may hold values from -6 to 6
- moe_grad: bfloat16 [32768, 2048], P(('ctx', 'exp')), may hold values from -60 to 60
- expert_ids: int32 [32768, 8], P(('ctx', 'exp')), may hold values from 0 to 127, all different within a row; in each aligned block of 128 rows (0 to 127, 128 to 255, ...) at most 10 rows name the same one
- keep_mask: int32 [32768, 8], P(('ctx', 'exp')), may hold values 0 or 1
- route_weight: float32 [32768, 8], P(('ctx', 'exp')), may hold values from 0.03 to 0.5
- w_gate: bfloat16 [16, 2048, 768], P('exp'), may hold values from -0.125 to 0.125
- w_up: bfloat16 [16, 2048, 768], P('exp'), may hold values from -0.125 to 0.125
- w_down: bfloat16 [16, 768, 2048], P('exp'), may hold values from -0.21875 to 0.21875
Outputs:
- grad_queries: bfloat16 [32768, 16, 128], P(('ctx', 'exp'))
- grad_keys: bfloat16 [32768, 2, 128], P(('ctx', 'exp'))
- grad_values: bfloat16 [32768, 2, 128], P(('ctx', 'exp'))
- grad_moe_input: bfloat16 [32768, 2048], P(('ctx', 'exp'))
Inputs may be any that keep to these rules, and one draw needn't show every extreme that they name: `span_order`: each span number appears once. `expert_ids`: the 8 ids of a row differ; within the rows of one device (aligned blocks of 128 rows) no expert is named by more than 10 rows, a bound that some block reaches.
All inputs are finite; a program needn't handle non-finite values. No bound on the sum of `keep_mask` on one device may be relied on, other than what follows from the above.
Results may differ from a plain program's by a relative error of at most 0.0058.
Values may be sent and summed in bfloat16 or wider, within the bound.
No kernel may reach another device: no remote copies, remote signals or barrier semaphores. Data moves between devices by JAX's collectives and lax.ppermute only.
A program may use at most 128 MiB of HBM per device.

v0:
```python
import math

import jax
import jax.numpy as jnp
from jax import lax
from jax.sharding import PartitionSpec as P

SLOT = 10


def dot_rows(left, right):
    return lax.dot_general(
        left, right, (((1,), (1,)), ((), ())), preferred_element_type=jnp.float32
    )


def dot_cols(left, right):
    return lax.dot_general(
        left, right, (((0,), (0,)), ((), ())), preferred_element_type=jnp.float32
    )


def row_positions(span_order, ctx_rows, local_rows, shard_rows):
    half_rows = shard_rows // 2
    slot_count = span_order.shape[0]
    slot_index = jnp.where(local_rows < half_rows, ctx_rows, slot_count - 1 - ctx_rows)
    slot_table = jnp.arange(slot_count, dtype=jnp.int32)
    span_number = jnp.sum(
        jnp.where(slot_index[:, None] == slot_table[None, :], span_order[None, :], 0), axis=1
    )
    return span_number * half_rows + local_rows % half_rows


def head_scores(group_rows, key_block, value_block, key_pos, score_scale):
    query_rows, grad_rows, norm_rows, inner_rows, query_pos = group_rows
    scores = dot_rows(query_rows, key_block) * score_scale
    visible = key_pos[None, :] <= query_pos[:, None]
    probs = jnp.where(visible, jnp.exp(scores - norm_rows[:, None]), 0.0)
    dprobs = dot_rows(grad_rows, value_block)
    dscores = probs * (dprobs - inner_rows[:, None])
    return (probs.astype(jnp.bfloat16), dscores.astype(jnp.bfloat16))


def block_query_grad(groups, key_block, value_block, key_pos, score_scale):
    parts = []
    for kv_head in range(len(groups)):
        probs_b, dscores_b = head_scores(
            groups[kv_head],
            key_block[:, kv_head, :],
            value_block[:, kv_head, :],
            key_pos,
            score_scale,
        )
        parts.append(
            jnp.dot(dscores_b, key_block[:, kv_head, :], preferred_element_type=jnp.float32)
            * score_scale
        )
    return tuple(parts)


def block_key_terms(groups, key_block, value_block, key_pos, score_scale):
    term_list = []
    for kv_head in range(len(groups)):
        probs_b, dscores_b = head_scores(
            groups[kv_head],
            key_block[:, kv_head, :],
            value_block[:, kv_head, :],
            key_pos,
            score_scale,
        )
        grad_key = dot_cols(dscores_b, groups[kv_head][0]) * score_scale
        grad_value = dot_cols(probs_b, groups[kv_head][1])
        term_list.append(jnp.concatenate([grad_key, grad_value], axis=1))
    return jnp.stack(term_list, axis=1)


def on_device(
    queries,
    key_tensor,
    value_tensor,
    out_grad,
    log_norm,
    out_dot,
    span_order,
    moe_input,
    moe_grad,
    expert_ids,
    keep_mask,
    route_weight,
    w_gate,
    w_up,
    w_down,
):
    shard_rows, head_count, head_size = queries.shape
    kv_heads = key_tensor.shape[1]
    group_width = head_count // kv_heads
    score_scale = 1.0 / math.sqrt(head_size)
    exp_count = lax.axis_size("exp")
    ctx_index = lax.axis_index("ctx")
    local_rows = jnp.arange(shard_rows, dtype=jnp.int32)
    query_pos = row_positions(
        span_order, jnp.zeros((shard_rows,), jnp.int32) + ctx_index, local_rows, shard_rows
    )
    all_keys, all_values = (
        lax.all_gather(key_tensor, "ctx", axis=0, tiled=True),
        lax.all_gather(value_tensor, "ctx", axis=0, tiled=True),
    )
    key_count = all_keys.shape[0]
    key_rows = jnp.arange(key_count, dtype=jnp.int32)
    key_pos = row_positions(span_order, key_rows // shard_rows, key_rows % shard_rows, shard_rows)
    groups = []
    for kv_head in range(kv_heads):
        low_head = kv_head * group_width
        high_head = low_head + group_width
        groups.append(
            (
                queries[:, low_head:high_head, :].reshape(-1, head_size),
                out_grad[:, low_head:high_head, :].reshape(-1, head_size),
                log_norm[:, low_head:high_head].reshape(-1),
                out_dot[:, low_head:high_head].reshape(-1),
                jnp.repeat(query_pos, group_width),
            )
        )
    query_parts = block_query_grad(groups, all_keys, all_values, key_pos, score_scale)
    terms_all = block_key_terms(groups, all_keys, all_values, key_pos, score_scale)
    summed = lax.psum_scatter(terms_all, "ctx", scatter_dimension=0, tiled=True)
    grad_queries = jnp.concatenate(
        [query_part.reshape(shard_rows, group_width, head_size) for query_part in query_parts],
        axis=1,
    ).astype(jnp.bfloat16)
    grad_keys = summed[:, :, :head_size].astype(jnp.bfloat16)
    grad_values = summed[:, :, head_size:].astype(jnp.bfloat16)
    token_rows, top_count = expert_ids.shape
    live_mask = (expert_ids < exp_count) & (keep_mask == 1)
    flat_ids = expert_ids.reshape(-1)
    flat_live = live_mask.reshape(-1)
    expert_table = jnp.arange(exp_count, dtype=jnp.int32)
    onehot = ((flat_ids[:, None] == expert_table[None, :]) & flat_live[:, None]).astype(jnp.int32)
    rank_ahead = jnp.cumsum(onehot, axis=0) - onehot
    position = jnp.sum(rank_ahead * onehot, axis=1)
    slot_of = jnp.where(flat_live, flat_ids * SLOT + position, -1).reshape(token_rows, top_count)
    slot_table = jnp.arange(exp_count * SLOT, dtype=jnp.int32)
    slot_hits = slot_of[None, :, :] == slot_table[:, None, None]
    dispatch = jnp.any(slot_hits, axis=2).astype(jnp.bfloat16)
    combine = jnp.sum(jnp.where(slot_hits, route_weight[None, :, :], 0.0), axis=2)
    send_inputs = (
        jnp.dot(dispatch, moe_input, preferred_element_type=jnp.float32)
        .astype(jnp.bfloat16)
        .reshape(exp_count, SLOT, -1)
    )
    send_grads = (
        jnp.dot(dispatch, moe_grad, preferred_element_type=jnp.float32)
        .astype(jnp.bfloat16)
        .reshape(exp_count, SLOT, -1)
    )
    inputs_in = lax.all_to_all(send_inputs, "exp", split_axis=0, concat_axis=0, tiled=True)
    grads_in = lax.all_to_all(send_grads, "exp", split_axis=0, concat_axis=0, tiled=True)
    sources, item_count, model_width = inputs_in.shape
    input_rows = inputs_in.reshape(-1, model_width)
    grad_rows = grads_in.reshape(-1, model_width)
    gate_pre = jnp.dot(input_rows, w_gate[0], preferred_element_type=jnp.float32)
    up_pre = jnp.dot(input_rows, w_up[0], preferred_element_type=jnp.float32)
    hidden_grad = dot_rows(grad_rows, w_down[0])
    sigmoid_gate = jax.nn.sigmoid(gate_pre)
    gate_grad = (
        hidden_grad * up_pre * sigmoid_gate * (1.0 + gate_pre * (1.0 - sigmoid_gate))
    ).astype(jnp.bfloat16)
    up_grad = (hidden_grad * gate_pre * sigmoid_gate).astype(jnp.bfloat16)
    slot_grad = (dot_rows(gate_grad, w_gate[0]) + dot_rows(up_grad, w_up[0])).astype(jnp.bfloat16)
    returned = lax.all_to_all(
        slot_grad.reshape(sources, item_count, model_width),
        "exp",
        split_axis=0,
        concat_axis=0,
        tiled=True,
    )
    flat_back = returned.reshape(exp_count * SLOT, -1).astype(jnp.float32)
    grad_moe = lax.dot_general(
        combine,
        flat_back,
        (((0,), (0,)), ((), ())),
        precision=lax.Precision.HIGHEST,
        preferred_element_type=jnp.float32,
    )
    return (grad_queries, grad_keys, grad_values, grad_moe.astype(jnp.bfloat16))


def solution(mesh):
    in_specs = (
        P(("ctx", "exp"), None, None),
        P(("ctx", "exp"), None, None),
        P(("ctx", "exp"), None, None),
        P(("ctx", "exp"), None, None),
        P(("ctx", "exp"), None),
        P(("ctx", "exp"), None),
        P(),
        P(("ctx", "exp"), None),
        P(("ctx", "exp"), None),
        P(("ctx", "exp"), None),
        P(("ctx", "exp"), None),
        P(("ctx", "exp"), None),
        P("exp", None, None),
        P("exp", None, None),
        P("exp", None, None),
    )
    out_specs = (
        P(("ctx", "exp"), None, None),
        P(("ctx", "exp"), None, None),
        P(("ctx", "exp"), None, None),
        P(("ctx", "exp"), None),
    )
    return jax.shard_map(
        on_device, mesh=mesh, in_specs=in_specs, out_specs=out_specs, check_vma=False
    )
```

profile of v0, /device:TPU:4, one launch (start us, length us, event | category | flops | bytes accessed | tf_op | source)
XLA Modules:
  0.0 273.5 jit_solution(4878055562834782876)
XLA Ops:
  7.2 1.6 copy.63
  8.9 1.5 copy.65
  10.5 0.8 copy.69
  11.3 0.7 compare_and_fusion
  12.0 0.7 fusion.88
  12.7 0.7 fusion.89
  13.4 0.1 copy.70
  13.5 0.1 and.81
  13.6 0.1 copy.66
  13.7 0.1 sub.90
  13.8 0.1 copy.64
  14.0 0.7 select_reduce_fusion.2
  14.9 0.1 le.9
  15.1 4.5 %reduce-window.6 = s32[16,8,128]{2,1,0:T(8,128)S(1)} reduce-window(s32[16,8,128]{2,1,0:T(8,128)S(1)} %fusion.69, s32[]{:T(128)} %constant.69.clone.1), window={size=1x1x128 pad=0_0x0_0x127_0}, to_apply=%region_3.4 | reduce-window | flops 2080768 | bytes 131076 | tf_op jit(solution)/shard_map/reduce-window
  19.7 0.1 copy.73
  19.9 0.1 copy.68
  20.0 0.1 sub.96
  20.1 0.1 copy.67
  20.3 0.8 select_reduce_fusion.1
  21.1 40.9 %all-gather.3.cloned.1.call-done = bf16[2048,2,128]{2,0,1:T(8,128)(2,1)} async-done(((bf16[128,2,128]{2,0,1:T(8,128)(2,1)}), bf16[2048,2,128]{2,0,1:T(8,128)(2,1)}) %all-gather.3.cloned.1.call-update) | async-done | bytes 1048592 | tf_op jit(solution)/shard_map/all_gather | solution.py:105
  62.0 2.4 fusion.45
  64.5 3.3 %copy-done.1 = f32[1024,2048]{1,0:T(8,128)} copy-done((f32[1024,2048]{1,0:T(8,128)}, f32[1024,2048]{1,0:T(8,128)S(1)}, u32[]{:S(2)}) %copy-start.1) | copy-done | bytes 8388632
  67.8 3.0 %fusion.2 = f32[2048,128]{0,1:T(8,128)} fusion(f32[1024,2048]{1,0:T(8,128)S(1)} %fusion.45, f32[1024]{0:T(1024)S(1)} %sub.93, s32[2048]{0:T(1024)S(1)} %fusion.77, s32[1024]{0:T(1024)S(1)} %le.9, bf16[128,16,128]{2,1,0:T(8,128)(2,1)S(1)} %copy-done.14), kind=kOutput, calls=%fused_computation.7 | convolution fusion | flops 547356672 | bytes 9715712 | tf_op jit(solution)/shard_map/dot_general | solution.py:18
  70.8 43.2 %all-gather.5.cloned.1.call-done = bf16[2048,2,128]{2,0,1:T(8,128)(2,1)} async-done(((bf16[128,2,128]{2,0,1:T(8,128)(2,1)}), bf16[2048,2,128]{2,0,1:T(8,128)(2,1)}) %all-gather.5.cloned.1.call-update) | async-done | bytes 1048592 | tf_op jit(solution)/shard_map/all_gather | solution.py:106
  114.0 5.3 %multiply_convert_fusion = bf16[1024,2048]{1,0:T(8,128)(2,1)S(1)} fusion(f32[1024,2048]{1,0:T(8,128)} %copy-done.1, f32[1024]{0:T(1024)S(1)} %sub.96, f32[1024]{0:T(1024)S(1)} %sub.93, s32[2048]{0:T(1024)S(1)} %fusion.77, s32[1024]{0:T(1024)S(1)} %le.9, bf16[2048,2,128]{2,0,1:T(8,128)(2,1)} %all-gather.5.cloned.1.call-done, bf16[128,16,128]{2,1,0:T(8,128)(2,1)} %param.18), kind=kOutput, calls=%fused_computation.2 | convolution fusion | flops 551550976 | bytes 13389824 | tf_op jit(solution)/shard_map/dot_general | solution.py:12
  119.3 2.0 copy-done.2
  121.4 0.8 convolution_multiply_fusion
  122.1 0.5 copy-done.8
  122.6 1.2 fusion.44
  123.9 2.0 fusion.4
  125.9 3.5 %multiply_convert_fusion.1 = bf16[1024,2048]{1,0:T(8,128)(2,1)S(1)} fusion(f32[1024,2048]{1,0:T(8,128)S(1)} %fusion.44, f32[1024]{0:T(1024)S(1)} %sub.90, f32[1024]{0:T(1024)S(1)} %sub.87, s32[2048]{0:T(1024)S(1)} %fusion.77, s32[1024]{0:T(1024)S(1)} %le.9, bf16[2048,2,128]{2,0,1:T(8,128)(2,1)S(1)} %copy-done.13, bf16[128,16,128]{2,1,0:T(8,128)(2,1)S(1)} %copy-done.15), kind=kOutput, calls=%fused_computation.3 | convolution fusion | flops 551550976 | bytes 13389824 | tf_op jit(solution)/shard_map/dot_general | solution.py:12
  129.4 0.8 convolution_multiply_fusion.1
  130.2 1.2 copy-done.10
  131.4 0.5 maximum_bitcast_fusion
  131.9 2.5 pad_maximum_fusion
  134.5 0.1 and.78
  134.9 0.2 copy-done.11
  135.1 0.2 fusion.40
  135.3 2.2 convolution_convert_fusion
  137.5 2.2 reshape.147
  139.7 8.3 %all-to-all-start.1 = ((bf16[16,10,2048]{2,1,0:T(8,128)(2,1)}), bf16[16,10,2048]{2,1,0:T(8,128)(2,1)}, u32[]{:S(2)}, u32[]{:S(2)}) async-start(bf16[16,10,2048]{2,1,0:T(8,128)(2,1)} %reshape.147), calls=%async_computation.2 | async-start | bytes 2097152 | tf_op jit(solution)/shard_map/all_to_all | solution.py:156
  148.0 2.3 convolution_convert_fusion.1
  150.2 2.2 reshape.145
  152.5 24.7 %all-to-all-done.1 = bf16[16,10,2048]{2,1,0:T(8,128)(2,1)} async-done(((bf16[16,10,2048]{2,1,0:T(8,128)(2,1)}), bf16[16,10,2048]{2,1,0:T(8,128)(2,1)}, u32[]{:S(2)}, u32[]{:S(2)}) %all-to-all-start.1) | async-done | bytes 655392 | tf_op jit(solution)/shard_map/all_to_all | solution.py:156
  177.2 4.3 %all-to-all-start = ((bf16[16,10,2048]{2,1,0:T(8,128)(2,1)}), bf16[16,10,2048]{2,1,0:T(8,128)(2,1)}, u32[]{:S(2)}, u32[]{:S(2)}) async-start(bf16[16,10,2048]{2,1,0:T(8,128)(2,1)} %reshape.145), calls=%async_computation.1 | async-start | bytes 2097152 | tf_op jit(solution)/shard_map/all_to_all | solution.py:157
  181.5 2.2 reshape.148
  183.7 24.1 %all-to-all-done = bf16[16,10,2048]{2,1,0:T(8,128)(2,1)} async-done(((bf16[16,10,2048]{2,1,0:T(8,128)(2,1)}), bf16[16,10,2048]{2,1,0:T(8,128)(2,1)}, u32[]{:S(2)}, u32[]{:S(2)}) %all-to-all-start) | async-done | bytes 655392 | tf_op jit(solution)/shard_map/all_to_all | solution.py:157
  207.8 2.2 reshape.146
  210.0 3.8 %fusion.8 = f32[160,768]{1,0:T(8,128)} fusion(bf16[160,2048]{1,0:T(8,128)(2,1)} %reshape.148, bf16[1,2048,768]{2,1,0:T(8,128)(2,1)} %param.27), kind=kOutput, calls=%fused_computation.11 | convolution fusion | flops 503316480 | bytes 4292608 | tf_op jit(solution)/shard_map/dot_general | solution.py:161
  213.8 2.0 fusion.14
  215.8 5.4 %fusion.6 = f32[160,2048]{1,0:T(8,128)} fusion(bf16[1,2048,768]{2,1,0:T(8,128)(2,1)} %param.27, f32[160,768]{1,0:T(8,128)} %fusion.14, bf16[160,2048]{1,0:T(8,128)(2,1)} %reshape.148, bf16[1,2048,768]{2,1,0:T(8,128)(2,1)S(1)} %copy-done, f32[160,768]{1,0:T(8,128)} %fusion.8), kind=kOutput, calls=%fused_computation.9 | convolution fusion | flops 1007861760 | bytes 9240576 | tf_op jit(solution)/shard_map/dot_general | solution.py:12
  221.1 3.6 %fusion.19 = bf16[160,2048]{1,0:T(8,128)(2,1)} fusion(f32[160,2048]{1,0:T(8,128)} %fusion.6, bf16[1,2048,768]{2,1,0:T(8,128)(2,1)S(1)} %copy-done, f32[160,768]{1,0:T(8,128)} %fusion.14, f32[160,768]{1,0:T(8,128)} %fusion.8), kind=kOutput, calls=%fused_computation.22 | convolution fusion | flops 504709120 | bytes 6094848 | tf_op jit(solution)/shard_map/dot_general | solution.py:12
  224.8 2.2 reshape.149
  227.0 4.3 %all-to-all-start.2 = ((bf16[16,10,2048]{2,1,0:T(8,128)(2,1)}), bf16[16,10,2048]{2,1,0:T(8,128)(2,1)}, u32[]{:S(2)}, u32[]{:S(2)}) async-start(bf16[16,10,2048]{2,1,0:T(8,128)(2,1)} %reshape.149), calls=%async_computation.3 | async-start | bytes 2097152 | tf_op jit(solution)/shard_map/all_to_all | solution.py:170
  231.4 0.2 select_reduce_fusion
  231.6 3.7 %fusion.36 = bf16[128,8,128]{2,1,0:T(8,128)(2,1)S(1)} fusion(bf16[1024,2048]{1,0:T(8,128)(2,1)} %copy-done.2, bf16[2048,2,128]{2,0,1:T(8,128)(2,1)} %all-gather.3.cloned.1.call-done), kind=kOutput, calls=%fused_computation.36 | convolution fusion | flops 537133056 | bytes 4980736 | tf_op jit(solution)/shard_map/dot_general | solution.py:55
  235.3 1.2 fusion.37
  236.6 0.9 pad_maximum_fusion.1
  237.5 22.3 %all-to-all-done.2 = bf16[16,10,2048]{2,1,0:T(8,128)(2,1)} async-done(((bf16[16,10,2048]{2,1,0:T(8,128)(2,1)}), bf16[16,10,2048]{2,1,0:T(8,128)(2,1)}, u32[]{:S(2)}, u32[]{:S(2)}) %all-to-all-start.2) | async-done | bytes 655392 | tf_op jit(solution)/shard_map/all_to_all | solution.py:170
  259.8 2.2 reshape.150
  262.0 2.5 convolution_convert_fusion.2
  264.5 1.0 convert.14
  265.5 0.8 copy.77
  266.2 0.8 copy.76
  (54 shorter events, 1.1 us)
Async XLA Ops:
  7.2 208.6 %copy-start = (bf16[1,2048,768]{2,1,0:T(8,128)(2,1)S(1)}, bf16[1,2048,768]{2,1,0:T(8,128)(2,1)}, u32[]{:S(2)}) copy-start(bf16[1,2048,768]{2,1,0:T(8,128)(2,1)} %param.28) | copy-start | bytes 9437188
  7.2 54.9 %all-gather.3.cloned.1.call-start = ((), (), s32[]{:S(2)}) async-start(), calls=%async_computation.4 | async-start | bytes 1114112 | tf_op jit(solution)/shard_map/all_gather | solution.py:105
  8.9 105.1 %all-gather.5.cloned.1.call-start = ((), (), s32[]{:S(2)}) async-start(), calls=%async_computation.5 | async-start | bytes 1114112 | tf_op jit(solution)/shard_map/all_gather | solution.py:106
  10.4 254.0 %reduce-scatter.2.cloned.1.call-start = ((), (), s32[]{:S(2)}) async-start(), calls=%async_computation.6 | async-start | bytes 4456448 | tf_op jit(solution)/shard_map/reduce_scatter | solution.py:126
  62.0 5.8 %copy-start.14 = (bf16[128,16,128]{2,1,0:T(8,128)(2,1)S(1)}, bf16[128,16,128]{2,1,0:T(8,128)(2,1)}, u32[]{:S(2)}) copy-start(bf16[128,16,128]{2,1,0:T(8,128)(2,1)} %param.18) | copy-start | bytes 1572868
  64.5 3.3 %copy-start.1 = (f32[1024,2048]{1,0:T(8,128)}, f32[1024,2048]{1,0:T(8,128)S(1)}, u32[]{:S(2)}) copy-start(f32[1024,2048]{1,0:T(8,128)S(1)} %fusion.45) | copy-start | bytes 25165828
  114.0 7.3 %copy-start.5 = (bf16[128,16,128]{2,1,0:T(8,128)(2,1)S(1)}, bf16[128,16,128]{2,1,0:T(8,128)(2,1)}, u32[]{:S(2)}) copy-start(bf16[128,16,128]{2,1,0:T(8,128)(2,1)} %param.15) | copy-start | bytes 1572868
  119.3 2.0 copy-start.2
  121.4 1.2 copy-start.8
  122.6 1.3 copy-start.15
  123.9 2.0 copy-start.13
  129.4 2.5 copy-start.3
  129.4 2.0 copy-start.10
  134.4 0.7 copy-start.11
  139.7 37.5 %all-to-all-start.1 = ((bf16[16,10,2048]{2,1,0:T(8,128)(2,1)}), bf16[16,10,2048]{2,1,0:T(8,128)(2,1)}, u32[]{:S(2)}, u32[]{:S(2)}) async-start(bf16[16,10,2048]{2,1,0:T(8,128)(2,1)} %reshape.147), calls=%async_computation.2 | async-start | bytes 2097152 | tf_op jit(solution)/shard_map/all_to_all | solution.py:156
  177.2 30.6 %all-to-all-start = ((bf16[16,10,2048]{2,1,0:T(8,128)(2,1)}), bf16[16,10,2048]{2,1,0:T(8,128)(2,1)}, u32[]{:S(2)}, u32[]{:S(2)}) async-start(bf16[16,10,2048]{2,1,0:T(8,128)(2,1)} %reshape.145), calls=%async_computation.1 | async-start | bytes 2097152 | tf_op jit(solution)/shard_map/all_to_all | solution.py:157
  210.0 3.8 %copy-start.6 = (bf16[1,768,2048]{2,1,0:T(8,128)(2,1)S(1)}, bf16[1,768,2048]{2,1,0:T(8,128)(2,1)}, u32[]{:S(2)}) copy-start(bf16[1,768,2048]{2,1,0:T(8,128)(2,1)} %param.29) | copy-start | bytes 9437188
  210.0 3.8 %copy-start.7 = (bf16[160,2048]{1,0:T(8,128)(2,1)S(1)}, bf16[160,2048]{1,0:T(8,128)(2,1)}, u32[]{:S(2)}) copy-start(bf16[160,2048]{1,0:T(8,128)(2,1)} %reshape.146) | copy-start | bytes 1966084
  221.1 10.2 %copy-start.12 = (f32[128,8]{0,1:T(8,128)S(1)}, f32[128,8]{0,1:T(8,128)}, u32[]{:S(2)}) copy-start(f32[128,8]{0,1:T(8,128)} %param.26) | copy-start | bytes 12292
  227.0 32.8 %all-to-all-start.2 = ((bf16[16,10,2048]{2,1,0:T(8,128)(2,1)}), bf16[16,10,2048]{2,1,0:T(8,128)(2,1)}, u32[]{:S(2)}, u32[]{:S(2)}) async-start(bf16[16,10,2048]{2,1,0:T(8,128)(2,1)} %reshape.149), calls=%async_computation.3 | async-start | bytes 2097152 | tf_op jit(solution)/shard_map/all_to_all | solution.py:170
  231.4 4.0 %copy-start.4 = (bf16[1024,2048]{1,0:T(8,128)(2,1)S(1)}, bf16[1024,2048]{1,0:T(8,128)(2,1)}, u32[]{:S(2)}) copy-start(bf16[1024,2048]{1,0:T(8,128)(2,1)} %copy-done.3) | copy-start | bytes 12582916
  231.4 4.0 %copy-start.9 = (bf16[2048,2,128]{2,0,1:T(8,128)(2,1)S(1)}, bf16[2048,2,128]{2,0,1:T(8,128)(2,1)}, u32[]{:S(2)}) copy-start(bf16[2048,2,128]{2,0,1:T(8,128)(2,1)} %all-gather.3.cloned.1.call-done) | copy-start | bytes 3145732
Sparse Core Ops, SparseCore 0:
  11.3 50.6 all-gather.2
  65.4 48.6 all-gather.4
  134.5 89.7 reduce-scatter.1
where the time goes:
time: 275 us; the launch traced here: 274 us
  waiting for transfers between devices  155 us (56%)
  matrix products  45.7 us (17%)
  local copies, waits for them, and re-layouts  29.1 us (11%)
  starting transfers between devices  17.1 us (6%)
  between operations  14.1 us (5%)
  other arithmetic  12.2 us (4%)
    all_gather x1, waiting for transfers between devices, on_device(): lax.all_gather(value_tensor, 'ctx', axis=0, tiled=True)  43.2 us
    all_gather x1, waiting for transfers between devices, on_device(): lax.all_gather(key_tensor, 'ctx', axis=0, tiled=True)  40.9 us
    all_to_all x1, waiting for transfers between devices, on_device(): lax.all_to_all(send_inputs, 'exp', split_axis=0, concat_axis=0, tiled=True)  24.7 us
    all_to_all x1, waiting for transfers between devices, on_device(): lax.all_to_all(send_grads, 'exp', split_axis=0, concat_axis=0, tiled=True)  24.1 us
    dot_general x7, matrix products, dot_rows(): lax.dot_general(left, right, (((1,), (1,)), ((), ())), preferred_element_...  23.4 us
    all_to_all x1, waiting for transfers between devices, on_device(): lax.all_to_all(slot_grad.reshape(sources, item_count, model_width), 'exp'...  22.3 us
    unnamed x37, local copies, waits for them, and re-layouts  12.7 us
    all_to_all x1, starting transfers between devices, on_device(): lax.all_to_all(send_inputs, 'exp', split_axis=0, concat_axis=0, tiled=True)  8.3 us
  transfers between devices with their start and end apart: 6, of which 5 were waited for; matrix products, arithmetic and copies ran while one was open for 22% of the time, Pallas kernels for 0%

commit v1 on v0

v1 whole, which is shorter than its diff:
```python
import functools
import math

import jax
import jax.numpy as jnp
from jax import lax
from jax.experimental import pallas as pl
from jax.experimental.pallas import tpu as pltpu
from jax.sharding import PartitionSpec as P

SLOT = 10
LANES = 128
CHUNK = 256
VMEM = pl.BlockSpec(memory_space=pltpu.VMEM)
SMEM = pl.BlockSpec(memory_space=pltpu.SMEM)
F32 = jnp.float32
BF16 = jnp.bfloat16


def dot(left, right):
    return jnp.dot(left, right, preferred_element_type=F32)


def dot_rows(left, right):
    return lax.dot_general(left, right, (((1,), (1,)), ((), ())), preferred_element_type=F32)


def dot_cols(left, right):
    return lax.dot_general(left, right, (((0,), (0,)), ((), ())), preferred_element_type=F32)


def attention_kernel(
    scale,
    kv_blocks,
    span_ref,
    chip_ref,
    q_own,
    q_got,
    d_own,
    d_got,
    stat_own,
    stat_got,
    *rest,
):
    kv_refs = rest[:kv_blocks]
    dq_own, dq_got, own_ref, part_ref = rest[kv_blocks : kv_blocks + 4]
    keys, values, keys_t, dk_acc, dv_acc, dq_acc = rest[kv_blocks + 4 :]
    chip = chip_ref[0]
    core = chip_ref[1]
    slots = span_ref.shape[0]
    half = keys.shape[0] // slots
    width = q_own.shape[1]
    repeat = width // half

    def span_of(chip_index, core_index, upper):
        place = chip_index * 2 + core_index
        return span_ref[slots - 1 - place if upper else place]

    for block in range(kv_blocks):
        for part in range(4):
            span = span_of(chip ^ block, part // 2, part % 2)
            at = pl.ds(pl.multiple_of(span * half, half), half)
            rows = kv_refs[block][part * half : (part + 1) * half, :]
            keys[at, :] = rows[:, :LANES]
            values[at, :] = rows[:, LANES:]
    chunks = keys.shape[0] // CHUNK
    for chunk in range(chunks):
        at = slice(chunk * CHUNK, (chunk + 1) * CHUNK)
        keys_t[chunk] = keys[at, :].T
    dk_acc[...] = jnp.zeros_like(dk_acc)
    dv_acc[...] = jnp.zeros_like(dv_acc)
    factor = scale / math.log(2.0)
    spans_in_chunk = CHUNK // half

    for index in range(4):
        upper = index % 2
        if index < 2:
            q_ref, d_ref, stat_ref, dq_ref, who = q_own, d_own, stat_own, dq_own, core
        else:
            q_ref, d_ref, stat_ref, dq_ref, who = q_got, d_got, stat_got, dq_got, 1 - core
        span = span_of(chip, who, upper)
        queries = q_ref[upper]
        grads = d_ref[upper]
        norm = stat_ref[0:1, upper * width : (upper + 1) * width] * (1.0 / math.log(2.0))
        inner = stat_ref[1:2, upper * width : (upper + 1) * width]
        dq_acc[...] = jnp.zeros_like(dq_acc)
        last = span // spans_in_chunk

        def one(chunk, masked):
            at = pl.ds(pl.multiple_of(chunk * CHUNK, CHUNK), CHUNK)
            key = keys[at, :]
            scores = dot_rows(key, queries)
            probs = jnp.exp2(scores * factor - norm)
            if masked:
                key_pos = chunk * CHUNK + lax.broadcasted_iota(jnp.int32, scores.shape, 0)
                query_pos = span * half + lax.broadcasted_iota(jnp.int32, scores.shape, 1) // repeat
                probs = jnp.where(key_pos <= query_pos, probs, 0.0)
            dprobs = dot_rows(values[at, :], grads)
            dscores = (probs * (dprobs - inner)).astype(BF16)
            dv_acc[at, :] += dot(probs.astype(BF16), grads)
            dk_acc[at, :] += dot(dscores, queries)
            dq_acc[...] += dot(keys_t[chunk], dscores)

        lax.fori_loop(0, last, lambda chunk, none: (one(chunk, False), none)[1], 0)
        one(last, True)
        dq_ref[upper] = (dq_acc[...].T * scale).astype(BF16)

    for block in range(kv_blocks):
        for part in range(4):
            span = span_of(chip ^ block, part // 2, part % 2)
            at = pl.ds(pl.multiple_of(span * half, half), half)
            rows = slice(part * half, (part + 1) * half)
            if block == 0:
                own_ref[rows, :LANES] = dk_acc[at, :] * scale
                own_ref[rows, LANES:] = dv_acc[at, :]
            else:
                part_ref[block - 1, rows, :LANES] = (dk_acc[at, :] * scale).astype(BF16)
                part_ref[block - 1, rows, LANES:] = dv_acc[at, :].astype(BF16)


def attention(span_order, place, q_own, q_got, d_own, d_got, stat_own, stat_got, kv_list, scale):
    blocks = len(kv_list)
    rows = kv_list[0].shape[0]
    total = blocks * rows
    spans, width, _ = q_own.shape
    return pl.pallas_call(
        functools.partial(attention_kernel, scale, blocks),
        out_shape=(
            jax.ShapeDtypeStruct(q_own.shape, BF16),
            jax.ShapeDtypeStruct(q_own.shape, BF16),
            jax.ShapeDtypeStruct((rows, 2 * LANES), F32),
            jax.ShapeDtypeStruct((blocks - 1, rows, 2 * LANES), BF16),
        ),
        in_specs=[SMEM, SMEM] + [VMEM] * (6 + blocks),
        out_specs=(VMEM,) * 4,
        scratch_shapes=[
            pltpu.VMEM((total, LANES), BF16),
            pltpu.VMEM((total, LANES), BF16),
            pltpu.VMEM((total // CHUNK, LANES, CHUNK), BF16),
            pltpu.VMEM((total, LANES), F32),
            pltpu.VMEM((total, LANES), F32),
            pltpu.VMEM((LANES, width), F32),
        ],
        compiler_params=pltpu.CompilerParams(vmem_limit_bytes=40 * 1024 * 1024),
        cost_estimate=pl.CostEstimate(
            flops=6 * spans * width * total * LANES * 2,
            bytes_accessed=6 * 1024 * 1024,
            transcendentals=spans * width * total,
        ),
        name="attention",
    )(span_order, place, q_own, q_got, d_own, d_got, stat_own, stat_got, *kv_list)


def slots_to_chunks(tiles, experts, blocks, chunk_ref, first):
    for expert in range(experts):
        for block in range(blocks):
            at = first + block * SLOT
            chunk_ref[expert, at : at + SLOT, :] = tiles[block, expert * SLOT : (expert + 1) * SLOT, :]


def dispatch_kernel(ids_ref, keep_ref, weight_ref, x_ref, g_ref, send_ref, combine_ref, tiles, chunks):
    rows, top = ids_ref.shape
    experts = send_ref.shape[0]
    blocks = x_ref.shape[1] // LANES
    slots = experts * SLOT
    column = lax.broadcasted_iota(jnp.int32, (rows, slots), 1)
    expert_of = column // SLOT
    slot_of = column - expert_of * SLOT
    ids = jnp.where(keep_ref[...] == 1, ids_ref[...], -1)
    weights = weight_ref[...]
    hit = jnp.zeros((rows, slots), F32)
    weight = jnp.zeros((rows, slots), F32)
    for k in range(top):
        match = ids[:, k : k + 1] == expert_of
        hit = jnp.where(match, 1.0, hit)
        weight = jnp.where(match, weights[:, k : k + 1], weight)
    earlier = (
        lax.broadcasted_iota(jnp.int32, (rows, rows), 1)
        < lax.broadcasted_iota(jnp.int32, (rows, rows), 0)
    ).astype(F32).astype(BF16)
    rank = dot(earlier, hit.astype(BF16))
    chosen = jnp.where(rank == slot_of.astype(F32), hit, 0.0)
    combine_ref[...] = chosen * weight
    pick = chosen.T.astype(BF16)
    for source, first in ((x_ref, 0), (g_ref, blocks * SLOT)):
        for pair in range(blocks // 2):
            both = dot(pick, source[:, pair * 2 * LANES : (pair + 1) * 2 * LANES])
            tiles[2 * pair] = both[:, :LANES]
            tiles[2 * pair + 1] = both[:, LANES:]
        slots_to_chunks(tiles, experts, blocks, chunks, first)
    send_ref[...] = chunks[...].astype(BF16)


def dispatch(ids, keep, weight, x, g, experts):
    rows = ids.shape[0]
    blocks = x.shape[1] // LANES
    slots = experts * SLOT
    return pl.pallas_call(
        dispatch_kernel,
        out_shape=(
            jax.ShapeDtypeStruct((experts, 2 * blocks * SLOT, LANES), BF16),
            jax.ShapeDtypeStruct((rows, slots), F32),
        ),
        in_specs=[VMEM] * 5,
        out_specs=(VMEM, VMEM),
        scratch_shapes=[
            pltpu.VMEM((blocks, slots, LANES), F32),
            pltpu.VMEM((experts, 2 * blocks * SLOT, LANES), F32),
        ],
        compiler_params=pltpu.CompilerParams(vmem_limit_bytes=32 * 1024 * 1024),
        name="dispatch",
    )(ids, keep, weight, x, g)


def mlp_kernel(in_ref, gate_ref, up_ref, down_ref, out_ref, chunks, tiles, x_rows, g_rows, total):
    sources = in_ref.shape[0]
    blocks = x_rows.shape[1] // LANES
    step = pl.program_id(0)

    @pl.when(step == 0)
    def _():
        chunks[...] = in_ref[...].astype(F32)
        for rows_ref, first in ((x_rows, 0), (g_rows, blocks * SLOT)):
            for block in range(blocks):
                for source in range(sources):
                    at = first + block * SLOT
                    tiles[block, source * SLOT : (source + 1) * SLOT, :] = chunks[source, at : at + SLOT, :]
                rows_ref[:, block * LANES : (block + 1) * LANES] = tiles[block].astype(BF16)
        total[...] = jnp.zeros_like(total)

    gate_w, up_w = gate_ref[0], up_ref[0]
    gate_pre = dot(x_rows[...], gate_w)
    up_pre = dot(x_rows[...], up_w)
    hidden = dot_rows(g_rows[...], down_ref[0])
    sig = jax.nn.sigmoid(gate_pre)
    gate_grad = (hidden * up_pre * sig * (1.0 + gate_pre * (1.0 - sig))).astype(BF16)
    up_grad = (hidden * gate_pre * sig).astype(BF16)
    total[...] += dot_rows(gate_grad, gate_w) + dot_rows(up_grad, up_w)

    @pl.when(step == pl.num_programs(0) - 1)
    def _():
        for block in range(blocks):
            tiles[block] = total[:, block * LANES : (block + 1) * LANES]
        slots_to_chunks(tiles, sources, blocks, chunks, 0)
        out_ref[...] = chunks[:, : blocks * SLOT, :].astype(BF16)


def mlp(received, w_gate, w_up, w_down):
    sources, chunk_rows, _ = received.shape
    _, width, hidden = w_gate.shape
    blocks = width // LANES
    tile = 256
    slots = sources * SLOT
    whole = lambda *shape: pl.BlockSpec(shape, lambda i: (0,) * len(shape))
    return pl.pallas_call(
        mlp_kernel,
        grid=(hidden // tile,),
        out_shape=jax.ShapeDtypeStruct((sources, blocks * SLOT, LANES), BF16),
        in_specs=[
            whole(sources, chunk_rows, LANES),
            pl.BlockSpec((1, width, tile), lambda i: (0, 0, i)),
            pl.BlockSpec((1, width, tile), lambda i: (0, 0, i)),
            pl.BlockSpec((1, tile, width), lambda i: (0, i, 0)),
        ],
        out_specs=whole(sources, blocks * SLOT, LANES),
        scratch_shapes=[
            pltpu.VMEM((sources, chunk_rows, LANES), F32),
            pltpu.VMEM((blocks, slots, LANES), F32),
            pltpu.VMEM((slots, width), BF16),
            pltpu.VMEM((slots, width), BF16),
            pltpu.VMEM((slots, width), F32),
        ],
        compiler_params=pltpu.CompilerParams(vmem_limit_bytes=40 * 1024 * 1024),
        cost_estimate=pl.CostEstimate(
            flops=10 * slots * width * hidden, bytes_accessed=11 * 1024 * 1024, transcendentals=slots * hidden
        ),
        name="experts",
    )(received, w_gate, w_up, w_down)


def combine_kernel(weight_ref, back_ref, out_ref, chunks, tiles):
    experts = back_ref.shape[0]
    blocks = out_ref.shape[1] // LANES
    chunks[...] = back_ref[...].astype(F32)
    weight = weight_ref[...]
    high = weight.astype(BF16)
    rest = weight - high.astype(F32)
    middle = rest.astype(BF16)
    low = (rest - middle.astype(F32)).astype(BF16)
    for block in range(blocks):
        for expert in range(experts):
            at = block * SLOT
            tiles[block, expert * SLOT : (expert + 1) * SLOT, :] = chunks[expert, at : at + SLOT, :]
    for pair in range(blocks // 2):
        rows = jnp.concatenate([tiles[2 * pair], tiles[2 * pair + 1]], axis=1).astype(BF16)
        out = dot(high, rows) + (dot(middle, rows) + dot(low, rows))
        out_ref[:, pair * 2 * LANES : (pair + 1) * 2 * LANES] = out.astype(BF16)


def combine(weight, back):
    experts, chunk_rows, _ = back.shape
    rows, slots = weight.shape
    blocks = chunk_rows // SLOT
    return pl.pallas_call(
        combine_kernel,
        out_shape=jax.ShapeDtypeStruct((rows, blocks * LANES), BF16),
        in_specs=[VMEM, VMEM],
        out_specs=VMEM,
        scratch_shapes=[
            pltpu.VMEM((experts, chunk_rows, LANES), F32),
            pltpu.VMEM((blocks, slots, LANES), F32),
        ],
        compiler_params=pltpu.CompilerParams(vmem_limit_bytes=32 * 1024 * 1024),
        name="combine",
    )(weight, back)


def on_device(
    queries,
    key_tensor,
    value_tensor,
    out_grad,
    log_norm,
    out_dot,
    span_order,
    moe_input,
    moe_grad,
    expert_ids,
    keep_mask,
    route_weight,
    w_gate,
    w_up,
    w_down,
):
    rows, heads, size = queries.shape
    group = heads // 2
    scale = 1.0 / math.sqrt(size)
    members = lax.axis_size("ctx")
    experts = lax.axis_size("exp")
    me = lax.axis_index("ctx")
    core = me % 2
    first = core == 0
    chips = members // 2
    swap = [(i, i ^ 1) for i in range(members)]

    send, weight = dispatch(expert_ids, keep_mask, route_weight, moe_input, moe_grad, experts)

    def halves(array):
        low, high = array[:, :group], array[:, group:]
        return jnp.where(first, low, high), jnp.where(first, high, low)

    q_own, q_away = halves(queries)
    d_own, d_away = halves(out_grad)
    stat_own, stat_away = halves(jnp.stack([log_norm, out_dot]).reshape(2 * rows, heads))
    kv = jnp.concatenate([key_tensor, value_tensor], axis=2)
    kv_own = jnp.where(first, kv[:, 0], kv[:, 1])
    kv_away = jnp.where(first, kv[:, 1], kv[:, 0])
    trade = lambda array: lax.ppermute(array, "ctx", swap)
    kv_got = trade(kv_away)
    q_got, d_got = trade(q_away), trade(d_away)
    stat_got = trade(stat_away.reshape(2, rows * group))
    kv_chip = jnp.concatenate([jnp.where(first, kv_own, kv_got), jnp.where(first, kv_got, kv_own)], axis=0)

    received = lax.all_to_all(send, "exp", split_axis=0, concat_axis=0, tiled=True)
    to_chip = lambda array, k: lax.ppermute(array, "ctx", [(i, i ^ (2 * k)) for i in range(members)])
    kv_list = [kv_chip] + [to_chip(kv_chip, k) for k in range(1, chips)]

    spans = lambda array: array.reshape(2, rows // 2 * group, size)
    place = jnp.stack([me // 2, core]).astype(jnp.int32)
    dq_own, dq_got, own_sum, parts = attention(
        span_order,
        place,
        spans(q_own),
        spans(q_got),
        spans(d_own),
        spans(d_got),
        stat_own.reshape(2, rows * group),
        stat_got,
        kv_list,
        scale,
    )
    slot_grad = mlp(received, w_gate, w_up, w_down)
    returned = lax.all_to_all(slot_grad, "exp", split_axis=0, concat_axis=0, tiled=True)

    total = own_sum
    for k in range(1, chips):
        total = total + to_chip(parts[k - 1], k).astype(F32)
    total = total.astype(BF16)
    low, high = total[:rows], total[rows:]
    kv_mine = jnp.where(first, low, high)
    kv_theirs = trade(jnp.where(first, high, low))
    dq_back = trade(dq_got)

    def joined(mine, theirs):
        return jnp.concatenate([jnp.where(first, mine, theirs), jnp.where(first, theirs, mine)], axis=1)

    grad_queries = joined(dq_own.reshape(rows, group, size), dq_back.reshape(rows, group, size))
    kv_grads = joined(kv_mine[:, None, :], kv_theirs[:, None, :])
    grad_moe = combine(weight, returned)
    return grad_queries, kv_grads[:, :, :size], kv_grads[:, :, size:], grad_moe


def solution(mesh):
    rows = P(("ctx", "exp"))
    in_specs = (rows,) * 6 + (P(),) + (rows,) * 5 + (P("exp"),) * 3
    return jax.shard_map(
        on_device, mesh=mesh, in_specs=in_specs, out_specs=(rows,) * 4, check_vma=False
    )
```

time: 275 us -> 126 us (0.46)
  waiting for transfers between devices: 155 us -> 24.4 us
  matrix products: 45.7 us -> 0 us
  starting transfers between devices: 17.1 us -> 53.7 us
  Pallas kernels: 0 us -> 20.9 us
  between operations: 14.1 us -> 1 us
  local copies, waits for them, and re-layouts: 29.1 us -> 20.8 us
  other arithmetic: 12.2 us -> 3.97 us
    all_gather x2 -> x0, waiting for transfers between devices: 84.1 us -> none  [the longest x1 43.2 us: on_device(): lax.all_gather(value_tensor, 'ctx', axis=0, tiled=True)]
    all_to_all x3 -> x2, waiting for transfers between devices: 71.2 us -> 9.94 us  [the longest x1 9.94 us: on_device(): lax.all_to_all(slot_grad, 'exp', split_axis=0, concat_axis=0, tiled=True)]
    dot_general x17 -> x0, matrix products: 45.7 us -> none  [the longest x7 23.4 us: dot_rows(): lax.dot_general(left, right, (((1,), (1,)), ((), ())), preferred_element_...]
    ppermute x0 -> x20, starting transfers between devices: none -> 32.5 us  [the longest x14 31.2 us: on_device(): lax.ppermute(array, 'ctx', [(i, i ^ 2 * k) for i in range(members)])]
    pallas_call x0 -> x4, Pallas kernels: none -> 20.9 us  [the longest x1 8.49 us: mlp(): pl.pallas_call(mlp_kernel, grid=(hidden // tile,), out_shape=jax.ShapeDty...]
    ppermute x0 -> x20, waiting for transfers between devices: none -> 14.5 us  [the longest x14 13.7 us: on_device(): lax.ppermute(array, 'ctx', [(i, i ^ 2 * k) for i in range(members)])]
    reshape x6 -> x2, local copies, waits for them, and re-layouts: 13.1 us -> 0.23 us  [the longest x1 0.12 us: on_device(): stat_got = trade(stat_away.reshape(2, rows * group))]
    another operation x6 -> x1, other arithmetic: 8.56 us -> 0.08 us  [on_device(): place = jnp.stack([me // 2, core]).astype(jnp.int32)]
  transfers between devices with their start and end apart: 6 -> 22, of which waited for: 5 -> 6; matrix products, arithmetic and copies ran while one was open for 22% -> 5% of each run, Pallas kernels for 0% -> 14%
where the time goes in v1:
time: 126 us; the launch traced here: 125 us
  starting transfers between devices  53.7 us (43%)
  waiting for transfers between devices  24.4 us (19%)
  Pallas kernels  20.9 us (17%)
  local copies, waits for them, and re-layouts  20.8 us (17%)
  other arithmetic  3.97 us (3%)
    ppermute x14, starting transfers between devices, on_device(): lax.ppermute(array, 'ctx', [(i, i ^ 2 * k) for i in range(members)])  31.2 us
    unnamed x58, local copies, waits for them, and re-layouts  20.3 us
    ppermute x14, waiting for transfers between devices, on_device(): lax.ppermute(array, 'ctx', [(i, i ^ 2 * k) for i in range(members)])  13.7 us
    all_to_all x1, starting transfers between devices, on_device(): lax.all_to_all(slot_grad, 'exp', split_axis=0, concat_axis=0, tiled=True)  12 us
    all_to_all x1, waiting for transfers between devices, on_device(): lax.all_to_all(slot_grad, 'exp', split_axis=0, concat_axis=0, tiled=True)  9.94 us
    all_to_all x1, starting transfers between devices, on_device(): lax.all_to_all(send, 'exp', split_axis=0, concat_axis=0, tiled=True)  9.21 us
    pallas_call x1, Pallas kernels, mlp(): pl.pallas_call(mlp_kernel, grid=(hidden // tile,), out_shape=jax.ShapeDty...  8.49 us
    pallas_call x1, Pallas kernels, attention(): pl.pallas_call(functools.partial(attention_kernel, scale, blocks), out_sh...  8.48 us
  transfers between devices with their start and end apart: 22, of which 6 were waited for; matrix products, arithmetic and copies ran while one was open for 5% of the time, Pallas kernels for 14%

profile of v1, /device:TPU:4, one launch (start us, length us, event | category | flops | bytes accessed | tf_op | source)
XLA Modules:
  0.0 124.8 jit_solution(1018709021147935324)
XLA Ops:
  0.7 0.8 copy.31.ids_ref
  1.5 0.8 copy.32.keep_ref
  2.3 0.8 copy.33.weight_ref
  3.1 1.0 copy-done.3
  4.1 1.0 copy-done.4
  5.2 2.4 %dispatch.1 = (bf16[16,320,128]{2,1,0:T(8,128)(2,1)}, f32[128,160]{1,0:T(8,128)S(1)}) custom-call(s32[128,8]{1,0:T(8,128)S(1)} %copy.31.ids_ref, s32[128,8]{1,0:T(8,128)S(1)} %copy.32.keep_ref, f32[128,8]{1,0:T(8,128)S(1)} %copy.33.weight_ref, bf16[128,2048]{1,0:T(8,128)(2,1)S(1)} %copy-done.3, bf16[128,2048]{1,0:T(8,128)(2,1)S(1)} %copy-done.4), custom_call_target="tpu_custom_call" | custom-call | tf_op jit(solution)/shard_map/dispatch/pallas_call | solution.py:198
  7.6 9.2 %all-to-all-start = ((bf16[16,320,128]{2,1,0:T(8,128)(2,1)}), bf16[16,320,128]{2,1,0:T(8,128)(2,1)S(1)}, u32[]{:S(2)}, u32[]{:S(2)}) async-start(bf16[16,320,128]{2,1,0:T(8,128)(2,1)} %get-tuple-element.15), calls=%async_computation | async-start | bytes 2621440 | tf_op jit(solution)/shard_map/all_to_all | solution.py:364
  16.9 0.1 collective-permute-start.3
  17.1 0.1 copy.28
  17.2 0.1 reshape.47
  17.3 0.6 collective-permute-start.2
  17.9 0.7 broadcast_select_fusion.2
  18.6 0.0 collective-permute-done.3
  18.7 3.3 %collective-permute-start.10 = (bf16[256,256]{1,0:T(8,128)(2,1)S(1)}, bf16[256,256]{1,0:T(8,128)(2,1)S(1)}, u32[]{:S(2)}, u32[]{:S(2)}) collective-permute-start(bf16[256,256]{1,0:T(8,128)(2,1)S(1)} %pad_maximum_fusion.1.rest_0_), channel_id=1, source_target_pairs={{0,224},{16,240},{32,192},{48,208},{64,160},{80,176},{96,128},{112... | collective-permute-start | bytes 393224 | tf_op jit(solution)/shard_map/ppermute | solution.py:365
  22.0 0.7 broadcast_select_fusion
  22.7 2.7 %collective-permute-start.4 = (bf16[256,256]{1,0:T(8,128)(2,1)S(1)}, bf16[256,256]{1,0:T(8,128)(2,1)S(1)}, u32[]{:S(2)}, u32[]{:S(2)}) collective-permute-start(bf16[256,256]{1,0:T(8,128)(2,1)S(1)} %pad_maximum_fusion.1.rest_0_), channel_id=1, source_target_pairs={{0,32},{16,48},{32,0},{48,16},{64,96},{80,112},{96,64},{112,80},{1... | collective-permute-start | bytes 393224 | tf_op jit(solution)/shard_map/ppermute | solution.py:365
  25.5 0.1 collective-permute-start.5
  25.6 2.1 %collective-permute-start.6 = (bf16[256,256]{1,0:T(8,128)(2,1)S(1)}, bf16[256,256]{1,0:T(8,128)(2,1)S(1)}, u32[]{:S(2)}, u32[]{:S(2)}) collective-permute-start(bf16[256,256]{1,0:T(8,128)(2,1)S(1)} %pad_maximum_fusion.1.rest_0_), channel_id=1, source_target_pairs={{0,96},{16,112},{32,64},{48,80},{64,32},{80,48},{96,0},{112,16},{1... | collective-permute-start | bytes 393224 | tf_op jit(solution)/shard_map/ppermute | solution.py:365
  27.7 1.1 collective-permute-done.10.rest_7_
  28.8 0.0 collective-permute-start.1
  28.8 4.0 %collective-permute-done.4.rest_1_ = bf16[256,256]{1,0:T(8,128)(2,1)S(1)} collective-permute-done((bf16[256,256]{1,0:T(8,128)(2,1)S(1)}, bf16[256,256]{1,0:T(8,128)(2,1)S(1)}, u32[]{:S(2)}, u32[]{:S(2)}) %collective-permute-start.4) | collective-permute-done | bytes 131104 | tf_op jit(solution)/shard_map/ppermute | solution.py:365
  32.8 0.6 copy-done.5
  33.5 0.4 collective-permute-start.7
  33.8 0.0 collective-permute-done.5.rest_2_
  33.8 3.7 %collective-permute-start.8 = (bf16[256,256]{1,0:T(8,128)(2,1)S(1)}, bf16[256,256]{1,0:T(8,128)(2,1)S(1)}, u32[]{:S(2)}, u32[]{:S(2)}) collective-permute-start(bf16[256,256]{1,0:T(8,128)(2,1)S(1)} %pad_maximum_fusion.1.rest_0_), channel_id=1, source_target_pairs={{0,160},{16,176},{32,128},{48,144},{64,224},{80,240},{96,192},{112... | collective-permute-start | bytes 393224 | tf_op jit(solution)/shard_map/ppermute | solution.py:365
  37.5 0.0 collective-permute-done.6.rest_3_
  37.6 0.1 copy.27
  37.7 0.1 reshape.46.stat_own
  37.8 0.1 pad_add_fusion.chip_ref
  37.9 2.7 %collective-permute-done.7.rest_4_ = bf16[256,256]{1,0:T(8,128)(2,1)S(1)} collective-permute-done((bf16[256,256]{1,0:T(8,128)(2,1)S(1)}, bf16[256,256]{1,0:T(8,128)(2,1)S(1)}, u32[]{:S(2)}, u32[]{:S(2)}) %collective-permute-start.7) | collective-permute-done | bytes 131104 | tf_op jit(solution)/shard_map/ppermute | solution.py:365
  40.6 0.6 copy-done.11
  41.2 6.0 %collective-permute-done.8.rest_5_ = bf16[256,256]{1,0:T(8,128)(2,1)S(1)} collective-permute-done((bf16[256,256]{1,0:T(8,128)(2,1)S(1)}, bf16[256,256]{1,0:T(8,128)(2,1)S(1)}, u32[]{:S(2)}, u32[]{:S(2)}) %collective-permute-start.8) | collective-permute-done | bytes 131104 | tf_op jit(solution)/shard_map/ppermute | solution.py:365
  47.2 0.7 copy-done.13
  47.8 0.7 copy-done.15
  48.5 0.9 copy-done.6
  49.4 0.9 copy-done.8
  50.3 0.9 copy-done.10
  51.2 0.9 copy-done.12
  52.1 0.9 copy-done.14
  53.0 0.9 copy-done.16
  54.0 0.7 copy-done.17
  54.6 8.5 %attention.1 = (bf16[2,512,128]{2,1,0:T(8,128)(2,1)S(1)}, bf16[2,512,128]{2,1,0:T(8,128)(2,1)S(1)}, f32[256,256]{1,0:T(8,128)S(1)}, bf16[7,256,256]{2,1,0:T(8,128)(2,1)S(1)}) custom-call(s32[32]{0:T(128)S(1)} %copy-done.17, s32[2]{0:T(128)S(1)} %pad_add_fusion.chip_ref, bf16[2,512,128]{2,1,0:T(8,128)(2,1)S(1)} %bitcast.38, ...), custom_call_target="tpu_custom_call" | custom-call | flops 3221225472 | bytes 6291456 | tf_op jit(solution)/shard_map/attention/pallas_call | solution.py:126
  63.1 0.1 slice_bitcast_fusion.6
  63.2 8.1 %collective-permute-start.12 = (bf16[256,256]{1,0:T(8,128)(2,1)S(1)}, bf16[256,256]{1,0:T(8,128)(2,1)S(1)}, u32[]{:S(2)}, u32[]{:S(2)}) collective-permute-start(bf16[256,256]{1,0:T(8,128)(2,1)S(1)} %get-tuple-element.24), channel_id=1, source_target_pairs={{0,32},{16,48},{32,0},{48,16},{64,96},{80,112},{96,64},{112,80},{1... | collective-permute-start | bytes 393224 | tf_op jit(solution)/shard_map/ppermute | solution.py:365
  71.3 1.6 %collective-permute-start.14 = (bf16[256,256]{1,0:T(8,128)(2,1)S(1)}, bf16[256,256]{1,0:T(8,128)(2,1)}, u32[]{:S(2)}, u32[]{:S(2)}) collective-permute-start(bf16[256,256]{1,0:T(8,128)(2,1)S(1)} %get-tuple-element.29), channel_id=1, source_target_pairs={{0,96},{16,112},{32,64},{48,80},{64,32},{80,48},{96,0},{112,16},{1... | collective-permute-start | bytes 393224 | tf_op jit(solution)/shard_map/ppermute | solution.py:365
  72.8 1.1 collective-permute-start.15
  73.9 5.3 %collective-permute-start.16 = (bf16[256,256]{1,0:T(8,128)(2,1)S(1)}, bf16[256,256]{1,0:T(8,128)(2,1)}, u32[]{:S(2)}, u32[]{:S(2)}) collective-permute-start(bf16[256,256]{1,0:T(8,128)(2,1)S(1)} %get-tuple-element.27), channel_id=1, source_target_pairs={{0,160},{16,176},{32,128},{48,144},{64,224},{80,240},{96,192},{112... | collective-permute-start | bytes 393224 | tf_op jit(solution)/shard_map/ppermute | solution.py:365
  79.2 1.2 collective-permute-start.17
  80.4 1.6 %collective-permute-start.18 = (bf16[256,256]{1,0:T(8,128)(2,1)S(1)}, bf16[256,256]{1,0:T(8,128)(2,1)}, u32[]{:S(2)}, u32[]{:S(2)}) collective-permute-start(bf16[256,256]{1,0:T(8,128)(2,1)S(1)} %get-tuple-element.25), channel_id=1, source_target_pairs={{0,224},{16,240},{32,192},{48,208},{64,160},{80,176},{96,128},{112... | collective-permute-start | bytes 393224 | tf_op jit(solution)/shard_map/ppermute | solution.py:365
  82.0 0.0 copy-start
  82.0 1.9 %copy-done = bf16[1,2048,768]{2,1,0:T(8,128)(2,1)S(1)} copy-done((bf16[1,2048,768]{2,1,0:T(8,128)(2,1)S(1)}, bf16[1,2048,768]{2,1,0:T(8,128)(2,1)}, u32[]{:S(2)}) %copy-start) | copy-done | bytes 3145752
  83.9 1.9 %copy-done.1 = bf16[1,2048,768]{2,1,0:T(8,128)(2,1)S(1)} copy-done((bf16[1,2048,768]{2,1,0:T(8,128)(2,1)S(1)}, bf16[1,2048,768]{2,1,0:T(8,128)(2,1)}, u32[]{:S(2)}) %copy-start.1) | copy-done | bytes 3145752
  85.8 1.9 %copy-done.2 = bf16[1,768,2048]{2,1,0:T(8,128)(2,1)S(1)} copy-done((bf16[1,768,2048]{2,1,0:T(8,128)(2,1)S(1)}, bf16[1,768,2048]{2,1,0:T(8,128)(2,1)}, u32[]{:S(2)}) %copy-start.2) | copy-done | bytes 3145752
  87.7 8.5 %experts.1 = bf16[16,160,128]{2,1,0:T(8,128)(2,1)} custom-call(bf16[16,320,128]{2,1,0:T(8,128)(2,1)S(1)} %all-to-all-done.in_ref, bf16[1,2048,768]{2,1,0:T(8,128)(2,1)S(1)} %copy-done, bf16[1,2048,768]{2,1,0:T(8,128)(2,1)S(1)} %copy-done.1, bf16[1,768,2048]{2,1,0:T(8,128)(2,1)S(1)} %copy-done.2), custom_call_target="tpu_custom_call" | custom-call | flops 2516582400 | bytes 11534336 | tf_op jit(solution)/shard_map/experts/pallas_call | solution.py:255
  96.2 12.0 %all-to-all-start.1 = ((bf16[16,160,128]{2,1,0:T(8,128)(2,1)}), bf16[16,160,128]{2,1,0:T(8,128)(2,1)S(1)}, u32[]{:S(2)}, u32[]{:S(2)}) async-start(bf16[16,160,128]{2,1,0:T(8,128)(2,1)} %experts.1), calls=%async_computation.1 | async-start | bytes 1310720 | tf_op jit(solution)/shard_map/all_to_all | solution.py:383
  108.2 1.4 %add_convert_fusion = bf16[256,256]{1,0:T(8,128)(2,1)S(1)} fusion(bf16[256,256]{1,0:T(8,128)(2,1)} %collective-permute-done.18, bf16[256,256]{1,0:T(8,128)(2,1)} %collective-permute-done.17, bf16[256,256]{1,0:T(8,128)(2,1)} %collective-permute-done.16, bf16[256,256]{1,0:T(8,128)(2,1)} %collective-permute-done.15, ...), kind=kLoop, calls=%fused_computation.1 | loop fusion | flops 983040 | bytes 1310720 | tf_op jit(solution)/shard_map/convert_element_type | solution.py:388
  109.7 0.1 collective-permute-start.19
  109.8 0.5 collective-permute-start.11
  110.2 0.7 collective-permute-done.19
  111.0 0.7 copy.34
  111.7 0.7 copy.35
  112.5 0.9 pad_maximum_fusion
  113.4 9.9 %all-to-all-done.1.back_ref = bf16[16,160,128]{2,1,0:T(8,128)(2,1)S(1)} async-done(((bf16[16,160,128]{2,1,0:T(8,128)(2,1)}), bf16[16,160,128]{2,1,0:T(8,128)(2,1)S(1)}, u32[]{:S(2)}, u32[]{:S(2)}) %all-to-all-start.1) | async-done | bytes 655392 | tf_op jit(solution)/shard_map/all_to_all | solution.py:383
  123.3 1.5 %combine.1 = bf16[128,2048]{1,0:T(8,128)(2,1)} custom-call(f32[128,160]{1,0:T(8,128)S(1)} %get-tuple-element.14.weight_ref, bf16[16,160,128]{2,1,0:T(8,128)(2,1)S(1)} %all-to-all-done.1.back_ref), custom_call_target="tpu_custom_call" | custom-call | tf_op jit(solution)/shard_map/combine/pallas_call | solution.py:304
  (62 shorter events, 0.3 us)
Async XLA Ops:
  0.6 16.2 %copy-start.22 = (bf16[128,2,128]{2,1,0:T(2,128)(2,1)S(1)}, bf16[128,2,128]{2,1,0:T(2,128)(2,1)}, u32[]{:S(2)}) copy-start(bf16[128,2,128]{2,1,0:T(2,128)(2,1)} %param.16) | copy-start | bytes 196612
  0.6 16.2 %copy-start.23 = (bf16[128,2,128]{2,1,0:T(2,128)(2,1)S(1)}, bf16[128,2,128]{2,1,0:T(2,128)(2,1)}, u32[]{:S(2)}) copy-start(bf16[128,2,128]{2,1,0:T(2,128)(2,1)} %param.17) | copy-start | bytes 196612
  0.7 16.4 %copy-start.25 = (f32[128,16]{0,1:T(8,128)S(1)}, f32[128,16]{0,1:T(8,128)}, u32[]{:S(2)}) copy-start(f32[128,16]{0,1:T(8,128)} %param.19) | copy-start | bytes 24580
  0.7 16.4 %copy-start.24 = (f32[128,16]{0,1:T(8,128)S(1)}, f32[128,16]{0,1:T(8,128)}, u32[]{:S(2)}) copy-start(f32[128,16]{0,1:T(8,128)} %param.20) | copy-start | bytes 24580
  3.1 1.0 copy-start.3
  4.1 1.0 copy-start.4
  5.2 12.7 %copy-start.18 = (bf16[128,16,128]{2,1,0:T(8,128)(2,1)S(1)}, bf16[128,16,128]{2,1,0:T(8,128)(2,1)}, u32[]{:S(2)}) copy-start(bf16[128,16,128]{2,1,0:T(8,128)(2,1)} %param.15) | copy-start | bytes 1572868
  5.2 16.8 %copy-start.19 = (bf16[128,16,128]{2,1,0:T(8,128)(2,1)S(1)}, bf16[128,16,128]{2,1,0:T(8,128)(2,1)}, u32[]{:S(2)}) copy-start(bf16[128,16,128]{2,1,0:T(8,128)(2,1)} %param.18) | copy-start | bytes 1572868
  7.6 74.4 %all-to-all-start = ((bf16[16,320,128]{2,1,0:T(8,128)(2,1)}), bf16[16,320,128]{2,1,0:T(8,128)(2,1)S(1)}, u32[]{:S(2)}, u32[]{:S(2)}) async-start(bf16[16,320,128]{2,1,0:T(8,128)(2,1)} %get-tuple-element.15), calls=%async_computation | async-start | bytes 2621440 | tf_op jit(solution)/shard_map/all_to_all | solution.py:364
  16.9 1.7 %collective-permute-start.3 = (bf16[128,256]{1,0:T(8,128)(2,1)S(1)}, bf16[128,256]{1,0:T(8,128)(2,1)S(1)}, u32[]{:S(2)}, u32[]{:S(2)}) collective-permute-start(bf16[128,256]{1,0:T(8,128)(2,1)S(1)} %select_bitcast_fusion.2), channel_id=1, source_target_pairs={{0,16},{16,0},{32,48},{48,32},{64,80},{80,64},{96,112},{112,96},{1... | collective-permute-start | bytes 196616 | tf_op jit(solution)/shard_map/ppermute | solution.py:358
  17.3 10.4 %collective-permute-start.2 = (f32[2,1024]{1,0:T(2,128)S(1)}, f32[2,1024]{1,0:T(2,128)S(1)}, u32[]{:S(2)}, u32[]{:S(2)}) collective-permute-start(f32[2,1024]{1,0:T(2,128)S(1)} %reshape.47), channel_id=1, source_target_pairs={{0,16},{16,0},{32,48},{48,32},{64,80},{80,64},{96,112},{112,96},{1... | collective-permute-start | bytes 24584 | tf_op jit(solution)/shard_map/ppermute | solution.py:358
  18.7 10.2 %collective-permute-start.10 = (bf16[256,256]{1,0:T(8,128)(2,1)S(1)}, bf16[256,256]{1,0:T(8,128)(2,1)S(1)}, u32[]{:S(2)}, u32[]{:S(2)}) collective-permute-start(bf16[256,256]{1,0:T(8,128)(2,1)S(1)} %pad_maximum_fusion.1.rest_0_), channel_id=1, source_target_pairs={{0,224},{16,240},{32,192},{48,208},{64,160},{80,176},{96,128},{112... | collective-permute-start | bytes 393224 | tf_op jit(solution)/shard_map/ppermute | solution.py:365
  22.7 10.1 %collective-permute-start.4 = (bf16[256,256]{1,0:T(8,128)(2,1)S(1)}, bf16[256,256]{1,0:T(8,128)(2,1)S(1)}, u32[]{:S(2)}, u32[]{:S(2)}) collective-permute-start(bf16[256,256]{1,0:T(8,128)(2,1)S(1)} %pad_maximum_fusion.1.rest_0_), channel_id=1, source_target_pairs={{0,32},{16,48},{32,0},{48,16},{64,96},{80,112},{96,64},{112,80},{1... | collective-permute-start | bytes 393224 | tf_op jit(solution)/shard_map/ppermute | solution.py:365
  25.5 8.4 %collective-permute-start.5 = (bf16[256,256]{1,0:T(8,128)(2,1)S(1)}, bf16[256,256]{1,0:T(8,128)(2,1)S(1)}, u32[]{:S(2)}, u32[]{:S(2)}) collective-permute-start(bf16[256,256]{1,0:T(8,128)(2,1)S(1)} %pad_maximum_fusion.1.rest_0_), channel_id=1, source_target_pairs={{0,64},{16,80},{32,96},{48,112},{64,0},{80,16},{96,32},{112,48},{1... | collective-permute-start | bytes 393224 | tf_op jit(solution)/shard_map/ppermute | solution.py:365
  25.6 11.9 %collective-permute-start.6 = (bf16[256,256]{1,0:T(8,128)(2,1)S(1)}, bf16[256,256]{1,0:T(8,128)(2,1)S(1)}, u32[]{:S(2)}, u32[]{:S(2)}) collective-permute-start(bf16[256,256]{1,0:T(8,128)(2,1)S(1)} %pad_maximum_fusion.1.rest_0_), channel_id=1, source_target_pairs={{0,96},{16,112},{32,64},{48,80},{64,32},{80,48},{96,0},{112,16},{1... | collective-permute-start | bytes 393224 | tf_op jit(solution)/shard_map/ppermute | solution.py:365
  27.7 20.8 %collective-permute-start = (bf16[128,8,128]{2,1,0:T(8,128)(2,1)}, bf16[128,8,128]{2,1,0:T(8,128)(2,1)S(1)}, u32[]{:S(2)}, u32[]{:S(2)}) collective-permute-start(bf16[128,8,128]{2,1,0:T(8,128)(2,1)} %get-tuple-element.35), channel_id=1, source_target_pairs={{0,16},{16,0},{32,48},{48,32},{64,80},{80,64},{96,112},{112,96},{1... | collective-permute-start | bytes 786440 | tf_op jit(solution)/shard_map/ppermute | solution.py:358
  28.8 19.7 %collective-permute-start.1 = (bf16[128,8,128]{2,1,0:T(8,128)(2,1)}, bf16[128,8,128]{2,1,0:T(8,128)(2,1)S(1)}, u32[]{:S(2)}, u32[]{:S(2)}) collective-permute-start(bf16[128,8,128]{2,1,0:T(8,128)(2,1)} %get-tuple-element.33), channel_id=1, source_target_pairs={{0,16},{16,0},{32,48},{48,32},{64,80},{80,64},{96,112},{112,96},{1... | collective-permute-start | bytes 786440 | tf_op jit(solution)/shard_map/ppermute | solution.py:358
  32.8 0.7 copy-start.5
  33.5 7.1 %collective-permute-start.7 = (bf16[256,256]{1,0:T(8,128)(2,1)S(1)}, bf16[256,256]{1,0:T(8,128)(2,1)S(1)}, u32[]{:S(2)}, u32[]{:S(2)}) collective-permute-start(bf16[256,256]{1,0:T(8,128)(2,1)S(1)} %pad_maximum_fusion.1.rest_0_), channel_id=1, source_target_pairs={{0,128},{16,144},{32,160},{48,176},{64,192},{80,208},{96,224},{112... | collective-permute-start | bytes 393224 | tf_op jit(solution)/shard_map/ppermute | solution.py:365
  33.8 14.7 %copy-start.7 = (bf16[256,256]{1,0:T(8,128)(2,1)}, bf16[256,256]{1,0:T(8,128)(2,1)S(1)}, u32[]{:S(2)}) copy-start(bf16[256,256]{1,0:T(8,128)(2,1)S(1)} %collective-permute-done.5.rest_2_) | copy-start | bytes 393220
  33.8 13.4 %collective-permute-start.8 = (bf16[256,256]{1,0:T(8,128)(2,1)S(1)}, bf16[256,256]{1,0:T(8,128)(2,1)S(1)}, u32[]{:S(2)}, u32[]{:S(2)}) collective-permute-start(bf16[256,256]{1,0:T(8,128)(2,1)S(1)} %pad_maximum_fusion.1.rest_0_), channel_id=1, source_target_pairs={{0,160},{16,176},{32,128},{48,144},{64,224},{80,240},{96,192},{112... | collective-permute-start | bytes 393224 | tf_op jit(solution)/shard_map/ppermute | solution.py:365
  37.5 11.0 %copy-start.9 = (bf16[256,256]{1,0:T(8,128)(2,1)}, bf16[256,256]{1,0:T(8,128)(2,1)S(1)}, u32[]{:S(2)}) copy-start(bf16[256,256]{1,0:T(8,128)(2,1)S(1)} %collective-permute-done.6.rest_3_) | copy-start | bytes 393220
  37.5 10.3 %collective-permute-start.9 = (bf16[256,256]{1,0:T(8,128)(2,1)S(1)}, bf16[256,256]{1,0:T(8,128)(2,1)S(1)}, u32[]{:S(2)}, u32[]{:S(2)}) collective-permute-start(bf16[256,256]{1,0:T(8,128)(2,1)S(1)} %pad_maximum_fusion.1.rest_0_), channel_id=1, source_target_pairs={{0,192},{16,208},{32,224},{48,240},{64,128},{80,144},{96,160},{112... | collective-permute-start | bytes 393224 | tf_op jit(solution)/shard_map/ppermute | solution.py:365
  40.6 0.6 copy-start.11
  47.2 0.7 copy-start.13
  47.8 0.7 copy-start.15
  48.5 0.9 copy-start.6
  49.4 0.9 copy-start.8
  50.3 0.9 copy-start.10
  51.2 0.9 copy-start.12
  52.1 0.9 copy-start.14
  53.0 0.9 copy-start.16
  54.0 0.7 copy-start.17
  63.2 16.0 %collective-permute-start.12 = (bf16[256,256]{1,0:T(8,128)(2,1)S(1)}, bf16[256,256]{1,0:T(8,128)(2,1)S(1)}, u32[]{:S(2)}, u32[]{:S(2)}) collective-permute-start(bf16[256,256]{1,0:T(8,128)(2,1)S(1)} %get-tuple-element.24), channel_id=1, source_target_pairs={{0,32},{16,48},{32,0},{48,16},{64,96},{80,112},{96,64},{112,80},{1... | collective-permute-start | bytes 393224 | tf_op jit(solution)/shard_map/ppermute | solution.py:365
  71.3 9.2 %collective-permute-start.13 = (bf16[256,256]{1,0:T(8,128)(2,1)S(1)}, bf16[256,256]{1,0:T(8,128)(2,1)S(1)}, u32[]{:S(2)}, u32[]{:S(2)}) collective-permute-start(bf16[256,256]{1,0:T(8,128)(2,1)S(1)} %get-tuple-element.30), channel_id=1, source_target_pairs={{0,64},{16,80},{32,96},{48,112},{64,0},{80,16},{96,32},{112,48},{1... | collective-permute-start | bytes 393224 | tf_op jit(solution)/shard_map/ppermute | solution.py:365
  71.3 36.9 %collective-permute-start.14 = (bf16[256,256]{1,0:T(8,128)(2,1)S(1)}, bf16[256,256]{1,0:T(8,128)(2,1)}, u32[]{:S(2)}, u32[]{:S(2)}) collective-permute-start(bf16[256,256]{1,0:T(8,128)(2,1)S(1)} %get-tuple-element.29), channel_id=1, source_target_pairs={{0,96},{16,112},{32,64},{48,80},{64,32},{80,48},{96,0},{112,16},{1... | collective-permute-start | bytes 393224 | tf_op jit(solution)/shard_map/ppermute | solution.py:365
  72.8 35.4 %collective-permute-start.15 = (bf16[256,256]{1,0:T(8,128)(2,1)S(1)}, bf16[256,256]{1,0:T(8,128)(2,1)}, u32[]{:S(2)}, u32[]{:S(2)}) collective-permute-start(bf16[256,256]{1,0:T(8,128)(2,1)S(1)} %get-tuple-element.28), channel_id=1, source_target_pairs={{0,128},{16,144},{32,160},{48,176},{64,192},{80,208},{96,224},{112... | collective-permute-start | bytes 393224 | tf_op jit(solution)/shard_map/ppermute | solution.py:365
  73.9 34.3 %collective-permute-start.16 = (bf16[256,256]{1,0:T(8,128)(2,1)S(1)}, bf16[256,256]{1,0:T(8,128)(2,1)}, u32[]{:S(2)}, u32[]{:S(2)}) collective-permute-start(bf16[256,256]{1,0:T(8,128)(2,1)S(1)} %get-tuple-element.27), channel_id=1, source_target_pairs={{0,160},{16,176},{32,128},{48,144},{64,224},{80,240},{96,192},{112... | collective-permute-start | bytes 393224 | tf_op jit(solution)/shard_map/ppermute | solution.py:365
  79.2 2.8 %copy-start.20 = (bf16[256,256]{1,0:T(8,128)(2,1)}, bf16[256,256]{1,0:T(8,128)(2,1)S(1)}, u32[]{:S(2)}) copy-start(bf16[256,256]{1,0:T(8,128)(2,1)S(1)} %collective-permute-done.12) | copy-start | bytes 393220
  79.2 29.0 %collective-permute-start.17 = (bf16[256,256]{1,0:T(8,128)(2,1)S(1)}, bf16[256,256]{1,0:T(8,128)(2,1)}, u32[]{:S(2)}, u32[]{:S(2)}) collective-permute-start(bf16[256,256]{1,0:T(8,128)(2,1)S(1)} %get-tuple-element.26), channel_id=1, source_target_pairs={{0,192},{16,208},{32,224},{48,240},{64,128},{80,144},{96,160},{112... | collective-permute-start | bytes 393224 | tf_op jit(solution)/shard_map/ppermute | solution.py:365
  80.4 1.6 %copy-start.21 = (bf16[256,256]{1,0:T(8,128)(2,1)}, bf16[256,256]{1,0:T(8,128)(2,1)S(1)}, u32[]{:S(2)}) copy-start(bf16[256,256]{1,0:T(8,128)(2,1)S(1)} %collective-permute-done.13) | copy-start | bytes 393220
  80.4 27.8 %collective-permute-start.18 = (bf16[256,256]{1,0:T(8,128)(2,1)S(1)}, bf16[256,256]{1,0:T(8,128)(2,1)}, u32[]{:S(2)}, u32[]{:S(2)}) collective-permute-start(bf16[256,256]{1,0:T(8,128)(2,1)S(1)} %get-tuple-element.25), channel_id=1, source_target_pairs={{0,224},{16,240},{32,192},{48,208},{64,160},{80,176},{96,128},{112... | collective-permute-start | bytes 393224 | tf_op jit(solution)/shard_map/ppermute | solution.py:365
  82.0 1.9 %copy-start = (bf16[1,2048,768]{2,1,0:T(8,128)(2,1)S(1)}, bf16[1,2048,768]{2,1,0:T(8,128)(2,1)}, u32[]{:S(2)}) copy-start(bf16[1,2048,768]{2,1,0:T(8,128)(2,1)} %gate_ref.1) | copy-start | bytes 9437188
  83.9 1.9 %copy-start.1 = (bf16[1,2048,768]{2,1,0:T(8,128)(2,1)S(1)}, bf16[1,2048,768]{2,1,0:T(8,128)(2,1)}, u32[]{:S(2)}) copy-start(bf16[1,2048,768]{2,1,0:T(8,128)(2,1)} %up_ref.1) | copy-start | bytes 9437188
  85.8 1.9 %copy-start.2 = (bf16[1,768,2048]{2,1,0:T(8,128)(2,1)S(1)}, bf16[1,768,2048]{2,1,0:T(8,128)(2,1)}, u32[]{:S(2)}) copy-start(bf16[1,768,2048]{2,1,0:T(8,128)(2,1)} %down_ref.1) | copy-start | bytes 9437188
  96.2 27.1 %all-to-all-start.1 = ((bf16[16,160,128]{2,1,0:T(8,128)(2,1)}), bf16[16,160,128]{2,1,0:T(8,128)(2,1)S(1)}, u32[]{:S(2)}, u32[]{:S(2)}) async-start(bf16[16,160,128]{2,1,0:T(8,128)(2,1)} %experts.1), calls=%async_computation.1 | async-start | bytes 1310720 | tf_op jit(solution)/shard_map/all_to_all | solution.py:383
  109.7 1.3 %collective-permute-start.19 = (bf16[128,256]{1,0:T(8,128)(2,1)S(1)}, bf16[128,256]{1,0:T(8,128)(2,1)S(1)}, u32[]{:S(2)}, u32[]{:S(2)}) collective-permute-start(bf16[128,256]{1,0:T(8,128)(2,1)S(1)} %broadcast_select_fusion.7), channel_id=1, source_target_pairs={{0,16},{16,0},{32,48},{48,32},{64,80},{80,64},{96,112},{112,96},{1... | collective-permute-start | bytes 196616 | tf_op jit(solution)/shard_map/ppermute | solution.py:358
  109.8 2.7 %collective-permute-start.11 = (bf16[2,512,128]{2,1,0:T(8,128)(2,1)S(1)}, bf16[2,512,128]{2,1,0:T(8,128)(2,1)S(1)}, u32[]{:S(2)}, u32[]{:S(2)}) collective-permute-start(bf16[2,512,128]{2,1,0:T(8,128)(2,1)S(1)} %get-tuple-element.11), channel_id=1, source_target_pairs={{0,16},{16,0},{32,48},{48,32},{64,80},{80,64},{96,112},{112,96},{1... | collective-permute-start | bytes 786440 | tf_op jit(solution)/shard_map/ppermute | solution.py:358

commit v2 on v1

--- a/solution.py
+++ b/solution.py
@@ -13,6 +13,7 @@
 CHUNK = 256
 VMEM = pl.BlockSpec(memory_space=pltpu.VMEM)
 SMEM = pl.BlockSpec(memory_space=pltpu.SMEM)
+ANY = pl.BlockSpec(memory_space=pl.ANY)
 F32 = jnp.float32
 BF16 = jnp.bfloat16
 
@@ -57,8 +58,8 @@
         return span_ref[slots - 1 - place if upper else place]
 
     for block in range(kv_blocks):
-        for part in range(4):
-            span = span_of(chip ^ block, part // 2, part % 2)
+        for part in range(8):
+            span = span_of(chip ^ (2 * block + part // 4), part // 2 % 2, part % 2)
             at = pl.ds(pl.multiple_of(span * half, half), half)
             rows = kv_refs[block][part * half : (part + 1) * half, :]
             keys[at, :] = rows[:, :LANES]
@@ -106,8 +107,8 @@
         dq_ref[upper] = (dq_acc[...].T * scale).astype(BF16)
 
     for block in range(kv_blocks):
-        for part in range(4):
-            span = span_of(chip ^ block, part // 2, part % 2)
+        for part in range(8):
+            span = span_of(chip ^ (2 * block + part // 4), part // 2 % 2, part % 2)
             at = pl.ds(pl.multiple_of(span * half, half), half)
             rows = slice(part * half, (part + 1) * half)
             if block == 0:
@@ -141,7 +142,7 @@
             pltpu.VMEM((total, LANES), F32),
             pltpu.VMEM((LANES, width), F32),
         ],
-        compiler_params=pltpu.CompilerParams(vmem_limit_bytes=40 * 1024 * 1024),
+        compiler_params=pltpu.CompilerParams(vmem_limit_bytes=16 * 1024 * 1024),
         cost_estimate=pl.CostEstimate(
             flops=6 * spans * width * total * LANES * 2,
             bytes_accessed=6 * 1024 * 1024,
@@ -158,31 +159,38 @@
             chunk_ref[expert, at : at + SLOT, :] = tiles[block, expert * SLOT : (expert + 1) * SLOT, :]
 
 
-def dispatch_kernel(ids_ref, keep_ref, weight_ref, x_ref, g_ref, send_ref, combine_ref, tiles, chunks):
-    rows, top = ids_ref.shape
+def dispatch_kernel(ids_ref, keep_ref, weight_ref, x_hbm, g_hbm, send_ref, combine_ref, x_ref, g_ref, tiles, chunks, sems):
+    loads = [
+        pltpu.make_async_copy(source, target, sems.at[i])
+        for i, (source, target) in enumerate(((x_hbm, x_ref), (g_hbm, g_ref)))
+    ]
+    for load in loads:
+        load.start()
+    top, rows = ids_ref.shape
     experts = send_ref.shape[0]
     blocks = x_ref.shape[1] // LANES
     slots = experts * SLOT
-    column = lax.broadcasted_iota(jnp.int32, (rows, slots), 1)
-    expert_of = column // SLOT
-    slot_of = column - expert_of * SLOT
+    line = lax.broadcasted_iota(jnp.int32, (slots, rows), 0)
+    expert_of = line // SLOT
+    slot_of = line - expert_of * SLOT
     ids = jnp.where(keep_ref[...] == 1, ids_ref[...], -1)
     weights = weight_ref[...]
-    hit = jnp.zeros((rows, slots), F32)
-    weight = jnp.zeros((rows, slots), F32)
+    hit = jnp.zeros((slots, rows), F32)
+    weight = jnp.zeros((slots, rows), F32)
     for k in range(top):
-        match = ids[:, k : k + 1] == expert_of
+        match = ids[k : k + 1, :] == expert_of
         hit = jnp.where(match, 1.0, hit)
-        weight = jnp.where(match, weights[:, k : k + 1], weight)
+        weight = jnp.where(match, weights[k : k + 1, :], weight)
     earlier = (
-        lax.broadcasted_iota(jnp.int32, (rows, rows), 1)
-        < lax.broadcasted_iota(jnp.int32, (rows, rows), 0)
+        lax.broadcasted_iota(jnp.int32, (rows, rows), 0)
+        < lax.broadcasted_iota(jnp.int32, (rows, rows), 1)
     ).astype(F32).astype(BF16)
-    rank = dot(earlier, hit.astype(BF16))
+    rank = dot(hit.astype(BF16), earlier)
     chosen = jnp.where(rank == slot_of.astype(F32), hit, 0.0)
     combine_ref[...] = chosen * weight
-    pick = chosen.T.astype(BF16)
-    for source, first in ((x_ref, 0), (g_ref, blocks * SLOT)):
+    pick = chosen.astype(BF16)
+    for load, source, first in ((loads[0], x_ref, 0), (loads[1], g_ref, blocks * SLOT)):
+        load.wait()
         for pair in range(blocks // 2):
             both = dot(pick, source[:, pair * 2 * LANES : (pair + 1) * 2 * LANES])
             tiles[2 * pair] = both[:, :LANES]
@@ -199,78 +207,87 @@
         dispatch_kernel,
         out_shape=(
             jax.ShapeDtypeStruct((experts, 2 * blocks * SLOT, LANES), BF16),
-            jax.ShapeDtypeStruct((rows, slots), F32),
+            jax.ShapeDtypeStruct((slots, rows), F32),
         ),
-        in_specs=[VMEM] * 5,
+        in_specs=[VMEM] * 3 + [ANY] * 2,
         out_specs=(VMEM, VMEM),
         scratch_shapes=[
+            pltpu.VMEM(x.shape, BF16),
+            pltpu.VMEM(g.shape, BF16),
             pltpu.VMEM((blocks, slots, LANES), F32),
             pltpu.VMEM((experts, 2 * blocks * SLOT, LANES), F32),
+            pltpu.SemaphoreType.DMA((2,)),
         ],
-        compiler_params=pltpu.CompilerParams(vmem_limit_bytes=32 * 1024 * 1024),
+        compiler_params=pltpu.CompilerParams(vmem_limit_bytes=12 * 1024 * 1024),
         name="dispatch",
-    )(ids, keep, weight, x, g)
-
-
-def mlp_kernel(in_ref, gate_ref, up_ref, down_ref, out_ref, chunks, tiles, x_rows, g_rows, total):
+    )(ids.T, keep.T, weight.T, x, g)
+
+
+def mlp_kernel(in_ref, *rest):
+    weights_hbm = rest[:3]
+    out_ref = rest[3]
+    weights = rest[4:7]
+    chunks, tiles, x_rows, g_rows, sems = rest[7:]
     sources = in_ref.shape[0]
     blocks = x_rows.shape[1] // LANES
-    step = pl.program_id(0)
-
-    @pl.when(step == 0)
-    def _():
-        chunks[...] = in_ref[...].astype(F32)
-        for rows_ref, first in ((x_rows, 0), (g_rows, blocks * SLOT)):
-            for block in range(blocks):
-                for source in range(sources):
-                    at = first + block * SLOT
-                    tiles[block, source * SLOT : (source + 1) * SLOT, :] = chunks[source, at : at + SLOT, :]
-                rows_ref[:, block * LANES : (block + 1) * LANES] = tiles[block].astype(BF16)
-        total[...] = jnp.zeros_like(total)
-
-    gate_w, up_w = gate_ref[0], up_ref[0]
-    gate_pre = dot(x_rows[...], gate_w)
-    up_pre = dot(x_rows[...], up_w)
-    hidden = dot_rows(g_rows[...], down_ref[0])
-    sig = jax.nn.sigmoid(gate_pre)
-    gate_grad = (hidden * up_pre * sig * (1.0 + gate_pre * (1.0 - sig))).astype(BF16)
-    up_grad = (hidden * gate_pre * sig).astype(BF16)
-    total[...] += dot_rows(gate_grad, gate_w) + dot_rows(up_grad, up_w)
-
-    @pl.when(step == pl.num_programs(0) - 1)
-    def _():
+    hidden = weights[0].shape[1]
+    tile = 256
+    loads = []
+    for step in range(hidden // tile):
+        part = slice(step * tile, (step + 1) * tile)
+        for i in range(3):
+            at = (slice(None), part) if i < 2 else (part, slice(None))
+            load = pltpu.make_async_copy(weights_hbm[i].at[(0,) + at], weights[i].at[at], sems.at[3 * step + i])
+            load.start()
+            loads.append(load)
+    chunks[...] = in_ref[...].astype(F32)
+    for rows_ref, first in ((x_rows, 0), (g_rows, blocks * SLOT)):
         for block in range(blocks):
-            tiles[block] = total[:, block * LANES : (block + 1) * LANES]
-        slots_to_chunks(tiles, sources, blocks, chunks, 0)
-        out_ref[...] = chunks[:, : blocks * SLOT, :].astype(BF16)
+            for source in range(sources):
+                at = first + block * SLOT
+                tiles[block, source * SLOT : (source + 1) * SLOT, :] = chunks[source, at : at + SLOT, :]
+            rows_ref[:, block * LANES : (block + 1) * LANES] = tiles[block].astype(BF16)
+    total = None
+    for step in range(hidden // tile):
+        for i in range(3):
+            loads[3 * step + i].wait()
+        part = slice(step * tile, (step + 1) * tile)
+        gate_w, up_w = weights[0][:, part], weights[1][:, part]
+        gate_pre = dot(x_rows[...], gate_w)
+        up_pre = dot(x_rows[...], up_w)
+        hidden_grad = dot_rows(g_rows[...], weights[2][part, :])
+        sig = jax.nn.sigmoid(gate_pre)
+        gate_grad = (hidden_grad * up_pre * sig * (1.0 + gate_pre * (1.0 - sig))).astype(BF16)
+        up_grad = (hidden_grad * gate_pre * sig).astype(BF16)
+        term = dot_rows(gate_grad, gate_w) + dot_rows(up_grad, up_w)
+        for block in range(blocks):
+            piece = term[:, block * LANES : (block + 1) * LANES]
+            tiles[block] = piece if step == 0 else tiles[block] + piece
+    slots_to_chunks(tiles, sources, blocks, chunks, 0)
+    out_ref[...] = chunks[:, : blocks * SLOT, :].astype(BF16)
 
 
 def mlp(received, w_gate, w_up, w_down):
     sources, chunk_rows, _ = received.shape
     _, width, hidden = w_gate.shape
     blocks = width // LANES
-    tile = 256
     slots = sources * SLOT
-    whole = lambda *shape: pl.BlockSpec(shape, lambda i: (0,) * len(shape))
     return pl.pallas_call(
         mlp_kernel,
-        grid=(hidden // tile,),
         out_shape=jax.ShapeDtypeStruct((sources, blocks * SLOT, LANES), BF16),
-        in_specs=[
-            whole(sources, chunk_rows, LANES),
-            pl.BlockSpec((1, width, tile), lambda i: (0, 0, i)),
-            pl.BlockSpec((1, width, tile), lambda i: (0, 0, i)),
-            pl.BlockSpec((1, tile, width), lambda i: (0, i, 0)),
-        ],
-        out_specs=whole(sources, blocks * SLOT, LANES),
+        in_specs=[VMEM] + [ANY] * 3,
+        out_specs=VMEM,
         scratch_shapes=[
+            pltpu.VMEM((width, hidden), BF16),
+            pltpu.VMEM((width, hidden), BF16),
+            pltpu.VMEM((hidden, width), BF16),
             pltpu.VMEM((sources, chunk_rows, LANES), F32),
             pltpu.VMEM((blocks, slots, LANES), F32),
             pltpu.VMEM((slots, width), BF16),
             pltpu.VMEM((slots, width), BF16),
-            pltpu.VMEM((slots, width), F32),
+            pltpu.SemaphoreType.DMA((9,)),
         ],
-        compiler_params=pltpu.CompilerParams(vmem_limit_bytes=40 * 1024 * 1024),
+        compiler_params=pltpu.CompilerParams(vmem_limit_bytes=28 * 1024 * 1024),
         cost_estimate=pl.CostEstimate(
             flops=10 * slots * width * hidden, bytes_accessed=11 * 1024 * 1024, transcendentals=slots * hidden
         ),
@@ -282,7 +299,7 @@
     experts = back_ref.shape[0]
     blocks = out_ref.shape[1] // LANES
     chunks[...] = back_ref[...].astype(F32)
-    weight = weight_ref[...]
+    weight = weight_ref[...].T
     high = weight.astype(BF16)
     rest = weight - high.astype(F32)
     middle = rest.astype(BF16)
@@ -299,7 +316,7 @@
 
 def combine(weight, back):
     experts, chunk_rows, _ = back.shape
-    rows, slots = weight.shape
+    slots, rows = weight.shape
     blocks = chunk_rows // SLOT
     return pl.pallas_call(
         combine_kernel,
@@ -310,7 +327,7 @@
             pltpu.VMEM((experts, chunk_rows, LANES), F32),
             pltpu.VMEM((blocks, slots, LANES), F32),
         ],
-        compiler_params=pltpu.CompilerParams(vmem_limit_bytes=32 * 1024 * 1024),
+        compiler_params=pltpu.CompilerParams(vmem_limit_bytes=12 * 1024 * 1024),
         name="combine",
     )(weight, back)
 
@@ -361,9 +378,11 @@
     stat_got = trade(stat_away.reshape(2, rows * group))
     kv_chip = jnp.concatenate([jnp.where(first, kv_own, kv_got), jnp.where(first, kv_got, kv_own)], axis=0)
 
+    neighbour = lambda array: lax.ppermute(array, "ctx", [(i, i ^ 2) for i in range(members)])
+    along_y = lambda array, k: lax.ppermute(array, "ctx", [(i, i ^ (4 * k)) for i in range(members)])
+    kv_pair = jnp.concatenate([kv_chip, neighbour(kv_chip)], axis=0)
     received = lax.all_to_all(send, "exp", split_axis=0, concat_axis=0, tiled=True)
-    to_chip = lambda array, k: lax.ppermute(array, "ctx", [(i, i ^ (2 * k)) for i in range(members)])
-    kv_list = [kv_chip] + [to_chip(kv_chip, k) for k in range(1, chips)]
+    kv_list = [kv_pair] + [along_y(kv_pair, k) for k in range(1, chips // 2)]
 
     spans = lambda array: array.reshape(2, rows // 2 * group, size)
     place = jnp.stack([me // 2, core]).astype(jnp.int32)
@@ -379,12 +398,14 @@
         kv_list,
         scale,
     )
+    received, parts = lax.optimization_barrier((received, parts))
     slot_grad = mlp(received, w_gate, w_up, w_down)
     returned = lax.all_to_all(slot_grad, "exp", split_axis=0, concat_axis=0, tiled=True)
 
     total = own_sum
-    for k in range(1, chips):
-        total = total + to_chip(parts[k - 1], k).astype(F32)
+    for k in range(1, chips // 2):
+        total = total + along_y(parts[k - 1], k).astype(F32)
+    total = total[: 2 * rows] + neighbour(total[2 * rows :].astype(BF16)).astype(F32)
     total = total.astype(BF16)
     low, high = total[:rows], total[rows:]
     kv_mine = jnp.where(first, low, high)

time: 126 us -> 114 us (0.905)
  starting transfers between devices: 53.7 us -> 33.1 us
  waiting for transfers between devices: 24.4 us -> 31.5 us
  local copies, waits for them, and re-layouts: 20.8 us -> 23.9 us
    ppermute x14 -> x8, starting transfers between devices: 31.2 us -> 14.8 us  [the longest x6 13.8 us: on_device(): lax.ppermute(array, 'ctx', [(i, i ^ 4 * k) for i in range(members)])]
    ppermute x14 -> x8, waiting for transfers between devices: 13.7 us -> 20.4 us  [the longest x2 13.2 us: on_device(): lax.ppermute(array, 'ctx', [(i, i ^ 2) for i in range(members)])]
    all_to_all x1, starting transfers between devices: 12 us -> 8.26 us  [on_device(): lax.all_to_all(slot_grad, 'exp', split_axis=0, concat_axis=0, tiled=True)]
    convert_element_type x1, other arithmetic: 1.39 us -> 0.03 us  [on_device(): total = total.astype(BF16)]
    unnamed x58 -> x59, local copies, waits for them, and re-layouts: 20.3 us -> 20.9 us
  transfers between devices with their start and end apart: 22 -> 16, of which waited for: 6 -> 6; matrix products, arithmetic and copies ran while one was open for 5% -> 6% of each run, Pallas kernels for 14% -> 16%
where the time goes in v2:
time: 114 us
  starting transfers between devices  33.1 us (29%)
  waiting for transfers between devices  31.5 us (28%)
  local copies, waits for them, and re-layouts  23.9 us (21%)
  Pallas kernels  21.5 us (19%)
  other arithmetic  2.78 us (2%)
    unnamed x59, local copies, waits for them, and re-layouts  20.9 us
    ppermute x6, starting transfers between devices, on_device(): lax.ppermute(array, 'ctx', [(i, i ^ 4 * k) for i in range(members)])  13.8 us
    ppermute x2, waiting for transfers between devices, on_device(): lax.ppermute(array, 'ctx', [(i, i ^ 2) for i in range(members)])  13.2 us
    all_to_all x1, waiting for transfers between devices, on_device(): lax.all_to_all(slot_grad, 'exp', split_axis=0, concat_axis=0, tiled=True)  10.6 us
    all_to_all x1, starting transfers between devices, on_device(): lax.all_to_all(send, 'exp', split_axis=0, concat_axis=0, tiled=True)  9.22 us
    pallas_call x1, Pallas kernels, mlp(): pl.pallas_call(mlp_kernel, out_shape=jax.ShapeDtypeStruct((sources, block...  8.86 us
    pallas_call x1, Pallas kernels, attention(): pl.pallas_call(functools.partial(attention_kernel, scale, blocks), out_sh...  8.78 us
    all_to_all x1, starting transfers between devices, on_device(): lax.all_to_all(slot_grad, 'exp', split_axis=0, concat_axis=0, tiled=True)  8.26 us
  transfers between devices with their start and end apart: 16, of which 6 were waited for; matrix products, arithmetic and copies ran while one was open for 6% of the time, Pallas kernels for 16%

profile of v2, /device:TPU:4, one launch (start us, length us, event | category | flops | bytes accessed | tf_op | source)
XLA Modules:
  0.0 113.7 jit_solution(6328218489239545047)
XLA Ops:
  0.6 1.0 copy-done.3
  1.7 1.0 copy-done.4
  2.7 0.7 copy-done.7
  3.4 0.7 copy-done.8
  4.1 0.7 copy-done.9
  4.8 2.3 %dispatch.1 = (bf16[16,320,128]{2,1,0:T(8,128)(2,1)}, f32[160,128]{1,0:T(8,128)S(1)}) custom-call(s32[8,128]{1,0:T(8,128)S(1)} %bitcast.35, s32[8,128]{1,0:T(8,128)S(1)} %bitcast.36, f32[8,128]{1,0:T(8,128)S(1)} %bitcast.37, bf16[128,2048]{1,0:T(8,128)(2,1)S(1)} %copy-done.3, bf16[128,2048]{1,0:T(8,128)(2,1)S(1)} %copy-done.4), custom_call_target="tpu_custom_call" | custom-call | tf_op jit(solution)/shard_map/dispatch/pallas_call | solution.py:206
  7.2 0.0 copy-start.21
  7.2 9.2 %all-to-all-start = ((bf16[16,320,128]{2,1,0:T(8,128)(2,1)}), bf16[16,320,128]{2,1,0:T(8,128)(2,1)S(1)}, u32[]{:S(2)}, u32[]{:S(2)}) async-start(bf16[16,320,128]{2,1,0:T(8,128)(2,1)} %get-tuple-element.15), calls=%async_computation | async-start | bytes 2621440 | tf_op jit(solution)/shard_map/all_to_all | solution.py:384
  16.5 0.1 copy.25
  16.6 0.1 reshape.47
  16.7 0.1 collective-permute-start.2
  16.9 0.6 collective-permute-start.3
  17.5 0.7 broadcast_select_fusion.2
  18.2 0.0 collective-permute-start
  18.2 0.1 collective-permute-done.3
  18.4 0.9 collective-permute-start.4
  19.3 0.7 broadcast_select_fusion
  20.0 0.1 collective-permute-start.1
  20.1 5.7 %collective-permute-done.4 = bf16[256,256]{1,0:T(8,128)(2,1)S(1)} collective-permute-done((bf16[256,256]{1,0:T(8,128)(2,1)S(1)}, bf16[256,256]{1,0:T(8,128)(2,1)S(1)}, u32[]{:S(2)}, u32[]{:S(2)}) %collective-permute-start.4) | collective-permute-done | bytes 131104 | tf_op jit(solution)/shard_map/ppermute | solution.py:381
  25.9 3.1 %collective-permute-start.7 = (bf16[512,256]{1,0:T(8,128)(2,1)S(1)}, bf16[512,256]{1,0:T(8,128)(2,1)S(1)}, u32[]{:S(2)}, u32[]{:S(2)}) collective-permute-start(bf16[512,256]{1,0:T(8,128)(2,1)S(1)} %pad_maximum_fusion.1.rest_0_), channel_id=1, source_target_pairs={{0,192},{16,208},{32,224},{48,240},{64,128},{80,144},{96,160},{112... | collective-permute-start | bytes 786440 | tf_op jit(solution)/shard_map/ppermute | solution.py:382
  29.0 0.6 collective-permute-start.6
  29.6 0.0 collective-permute-done.2.stat_got
  29.6 0.5 collective-permute-start.5
  30.0 0.8 copy.24
  30.8 1.0 reshape.46.stat_own
  31.9 0.1 pad_add_fusion.chip_ref
  31.9 0.0 collective-permute-done
  31.9 0.7 copy-done.10
  32.6 0.7 copy-done.12
  33.3 7.2 %collective-permute-done.7.rest_3_ = bf16[512,256]{1,0:T(8,128)(2,1)S(1)} collective-permute-done((bf16[512,256]{1,0:T(8,128)(2,1)S(1)}, bf16[512,256]{1,0:T(8,128)(2,1)S(1)}, u32[]{:S(2)}, u32[]{:S(2)}) %collective-permute-start.7) | collective-permute-done | bytes 262176 | tf_op jit(solution)/shard_map/ppermute | solution.py:382
  40.5 0.7 copy-done.14
  41.2 0.7 copy-done.17
  41.9 0.7 copy-done.19
  42.6 0.9 copy-done.11
  43.6 0.9 copy-done.13
  44.5 0.9 copy-done.15
  45.5 0.9 copy-done.18
  46.4 0.9 copy-done.20
  47.4 8.8 %attention.1 = (bf16[2,512,128]{2,1,0:T(8,128)(2,1)S(1)}, bf16[2,512,128]{2,1,0:T(8,128)(2,1)S(1)}, f32[512,256]{1,0:T(8,128)S(1)}, bf16[3,512,256]{2,1,0:T(8,128)(2,1)S(1)}) custom-call(s32[32]{0:T(128)S(1)} %copy-done.21, s32[2]{0:T(128)S(1)} %pad_add_fusion.chip_ref, bf16[2,512,128]{2,1,0:T(8,128)(2,1)S(1)} %bitcast.33, ...), custom_call_target="tpu_custom_call" | custom-call | flops 3221225472 | bytes 6291456 | tf_op jit(solution)/shard_map/attention/pallas_call | solution.py:127
  56.2 0.0 copy-start.5
  56.2 0.7 copy-done.5
  56.9 0.7 copy-done.16
  57.6 0.0 all-to-all-done.in_ref
  57.6 0.9 slice_bitcast_fusion.2
  58.5 8.2 %collective-permute-start.11 = (bf16[512,256]{1,0:T(8,128)(2,1)}, bf16[512,256]{1,0:T(8,128)(2,1)S(1)}, u32[]{:S(2)}, u32[]{:S(2)}) collective-permute-start(bf16[512,256]{1,0:T(8,128)(2,1)} %get-tuple-element.29), channel_id=1, source_target_pairs={{0,192},{16,208},{32,224},{48,240},{64,128},{80,144},{96,160},{112... | collective-permute-start | bytes 786440 | tf_op jit(solution)/shard_map/ppermute | solution.py:382
  66.7 1.5 %collective-permute-start.10 = (bf16[512,256]{1,0:T(8,128)(2,1)}, bf16[512,256]{1,0:T(8,128)(2,1)S(1)}, u32[]{:S(2)}, u32[]{:S(2)}) collective-permute-start(bf16[512,256]{1,0:T(8,128)(2,1)} %get-tuple-element.30), channel_id=1, source_target_pairs={{0,128},{16,144},{32,160},{48,176},{64,192},{80,208},{96,224},{112... | collective-permute-start | bytes 786440 | tf_op jit(solution)/shard_map/ppermute | solution.py:382
  68.1 0.0 collective-permute-start.8
  68.1 1.9 %copy-done = bf16[1,2048,768]{2,1,0:T(8,128)(2,1)S(1)} copy-done((bf16[1,2048,768]{2,1,0:T(8,128)(2,1)S(1)}, bf16[1,2048,768]{2,1,0:T(8,128)(2,1)}, u32[]{:S(2)}) %copy-start) | copy-done | bytes 3145752
  70.0 1.9 %copy-done.1 = bf16[1,2048,768]{2,1,0:T(8,128)(2,1)S(1)} copy-done((bf16[1,2048,768]{2,1,0:T(8,128)(2,1)S(1)}, bf16[1,2048,768]{2,1,0:T(8,128)(2,1)}, u32[]{:S(2)}) %copy-start.1) | copy-done | bytes 3145752
  71.9 1.9 %copy-done.2 = bf16[1,768,2048]{2,1,0:T(8,128)(2,1)S(1)} copy-done((bf16[1,768,2048]{2,1,0:T(8,128)(2,1)S(1)}, bf16[1,768,2048]{2,1,0:T(8,128)(2,1)}, u32[]{:S(2)}) %copy-start.2) | copy-done | bytes 3145752
  73.8 8.9 %experts.1 = bf16[16,160,128]{2,1,0:T(8,128)(2,1)} custom-call(bf16[16,320,128]{2,1,0:T(8,128)(2,1)S(1)} %all-to-all-done.in_ref, bf16[1,2048,768]{2,1,0:T(8,128)(2,1)S(1)} %copy-done, bf16[1,2048,768]{2,1,0:T(8,128)(2,1)S(1)} %copy-done.1, bf16[1,768,2048]{2,1,0:T(8,128)(2,1)S(1)} %copy-done.2), custom_call_target="tpu_custom_call" | custom-call | flops 2516582400 | bytes 11534336 | tf_op jit(solution)/shard_map/experts/pallas_call | solution.py:275
  82.7 0.0 copy-start.6
  82.7 8.3 %all-to-all-start.1 = ((bf16[16,160,128]{2,1,0:T(8,128)(2,1)}), bf16[16,160,128]{2,1,0:T(8,128)(2,1)S(1)}, u32[]{:S(2)}, u32[]{:S(2)}) async-start(bf16[16,160,128]{2,1,0:T(8,128)(2,1)} %experts.1), calls=%async_computation.1 | async-start | bytes 1310720 | tf_op jit(solution)/shard_map/all_to_all | solution.py:403
  91.0 0.0 collective-permute-done.9
  91.0 0.1 convert_add_fusion
  91.2 0.1 collective-permute-start.12
  91.3 7.5 %collective-permute-done.12 = bf16[256,256]{1,0:T(8,128)(2,1)S(1)} collective-permute-done((bf16[256,256]{1,0:T(8,128)(2,1)S(1)}, bf16[256,256]{1,0:T(8,128)(2,1)S(1)}, u32[]{:S(2)}, u32[]{:S(2)}) %collective-permute-start.12) | collective-permute-done | bytes 131104 | tf_op jit(solution)/shard_map/ppermute | solution.py:381
  98.9 0.1 collective-permute-start.13
  99.0 0.9 pad_maximum_fusion
  99.9 0.4 collective-permute-done.13
  100.3 0.7 copy.29
  101.0 0.7 copy.28
  101.7 10.6 %all-to-all-done.1.back_ref = bf16[16,160,128]{2,1,0:T(8,128)(2,1)S(1)} async-done(((bf16[16,160,128]{2,1,0:T(8,128)(2,1)}), bf16[16,160,128]{2,1,0:T(8,128)(2,1)S(1)}, u32[]{:S(2)}, u32[]{:S(2)}) %all-to-all-start.1) | async-done | bytes 655392 | tf_op jit(solution)/shard_map/all_to_all | solution.py:403
  112.2 1.5 %combine.1 = bf16[128,2048]{1,0:T(8,128)(2,1)} custom-call(f32[160,128]{1,0:T(8,128)S(1)} %get-tuple-element.18.weight_ref, bf16[16,160,128]{2,1,0:T(8,128)(2,1)S(1)} %all-to-all-done.1.back_ref), custom_call_target="tpu_custom_call" | custom-call | tf_op jit(solution)/shard_map/combine/pallas_call | solution.py:321
  (54 shorter events, 0.3 us)
Async XLA Ops:
  0.6 1.0 copy-start.3
  1.7 1.0 copy-start.4
  2.7 0.7 copy-start.7
  3.4 0.7 copy-start.8
  4.1 0.7 copy-start.9
  4.8 11.6 %copy-start.26 = (f32[128,16]{0,1:T(8,128)S(1)}, f32[128,16]{0,1:T(8,128)}, u32[]{:S(2)}) copy-start(f32[128,16]{0,1:T(8,128)} %param.20) | copy-start | bytes 24580
  4.8 11.6 %copy-start.27 = (f32[128,16]{0,1:T(8,128)S(1)}, f32[128,16]{0,1:T(8,128)}, u32[]{:S(2)}) copy-start(f32[128,16]{0,1:T(8,128)} %param.19) | copy-start | bytes 24580
  4.8 12.0 %copy-start.24 = (bf16[128,2,128]{2,1,0:T(2,128)(2,1)S(1)}, bf16[128,2,128]{2,1,0:T(2,128)(2,1)}, u32[]{:S(2)}) copy-start(bf16[128,2,128]{2,1,0:T(2,128)(2,1)} %param.16) | copy-start | bytes 196612
  4.8 12.1 %copy-start.25 = (bf16[128,2,128]{2,1,0:T(2,128)(2,1)S(1)}, bf16[128,2,128]{2,1,0:T(2,128)(2,1)}, u32[]{:S(2)}) copy-start(bf16[128,2,128]{2,1,0:T(2,128)(2,1)} %param.17) | copy-start | bytes 196612
  4.8 12.7 %copy-start.22 = (bf16[128,16,128]{2,1,0:T(8,128)(2,1)S(1)}, bf16[128,16,128]{2,1,0:T(8,128)(2,1)}, u32[]{:S(2)}) copy-start(bf16[128,16,128]{2,1,0:T(8,128)(2,1)} %param.15) | copy-start | bytes 1572868
  4.8 14.5 %copy-start.23 = (bf16[128,16,128]{2,1,0:T(8,128)(2,1)S(1)}, bf16[128,16,128]{2,1,0:T(8,128)(2,1)}, u32[]{:S(2)}) copy-start(bf16[128,16,128]{2,1,0:T(8,128)(2,1)} %param.18) | copy-start | bytes 1572868
  7.2 35.5 %copy-start.21 = (s32[32]{0:T(128)S(1)}, s32[32]{0:T(128)}, u32[]{:S(2)}) copy-start(s32[32]{0:T(128)} %span_ref.1) | copy-start | bytes 388
  7.2 50.4 %all-to-all-start = ((bf16[16,320,128]{2,1,0:T(8,128)(2,1)}), bf16[16,320,128]{2,1,0:T(8,128)(2,1)S(1)}, u32[]{:S(2)}, u32[]{:S(2)}) async-start(bf16[16,320,128]{2,1,0:T(8,128)(2,1)} %get-tuple-element.15), calls=%async_computation | async-start | bytes 2621440 | tf_op jit(solution)/shard_map/all_to_all | solution.py:384
  16.7 12.9 %collective-permute-start.2 = (f32[2,1024]{1,0:T(2,128)S(1)}, f32[2,1024]{1,0:T(2,128)S(1)}, u32[]{:S(2)}, u32[]{:S(2)}) collective-permute-start(f32[2,1024]{1,0:T(2,128)S(1)} %reshape.47), channel_id=1, source_target_pairs={{0,16},{16,0},{32,48},{48,32},{64,80},{80,64},{96,112},{112,96},{1... | collective-permute-start | bytes 24584 | tf_op jit(solution)/shard_map/ppermute | solution.py:375
  16.9 1.5 %collective-permute-start.3 = (bf16[128,256]{1,0:T(8,128)(2,1)S(1)}, bf16[128,256]{1,0:T(8,128)(2,1)S(1)}, u32[]{:S(2)}, u32[]{:S(2)}) collective-permute-start(bf16[128,256]{1,0:T(8,128)(2,1)S(1)} %select_bitcast_fusion.2), channel_id=1, source_target_pairs={{0,16},{16,0},{32,48},{48,32},{64,80},{80,64},{96,112},{112,96},{1... | collective-permute-start | bytes 196616 | tf_op jit(solution)/shard_map/ppermute | solution.py:375
  18.2 13.7 %collective-permute-start = (bf16[128,8,128]{2,1,0:T(8,128)(2,1)}, bf16[128,8,128]{2,1,0:T(8,128)(2,1)S(1)}, u32[]{:S(2)}, u32[]{:S(2)}) collective-permute-start(bf16[128,8,128]{2,1,0:T(8,128)(2,1)} %get-tuple-element.35), channel_id=1, source_target_pairs={{0,16},{16,0},{32,48},{48,32},{64,80},{80,64},{96,112},{112,96},{1... | collective-permute-start | bytes 786440 | tf_op jit(solution)/shard_map/ppermute | solution.py:375
  18.4 7.4 %collective-permute-start.4 = (bf16[256,256]{1,0:T(8,128)(2,1)S(1)}, bf16[256,256]{1,0:T(8,128)(2,1)S(1)}, u32[]{:S(2)}, u32[]{:S(2)}) collective-permute-start(bf16[256,256]{1,0:T(8,128)(2,1)S(1)} %pad_maximum_fusion.2), channel_id=1, source_target_pairs={{0,32},{16,48},{32,0},{48,16},{64,96},{80,112},{96,64},{112,80},{1... | collective-permute-start | bytes 393224 | tf_op jit(solution)/shard_map/ppermute | solution.py:381
  20.0 12.6 %collective-permute-start.1 = (bf16[128,8,128]{2,1,0:T(8,128)(2,1)}, bf16[128,8,128]{2,1,0:T(8,128)(2,1)S(1)}, u32[]{:S(2)}, u32[]{:S(2)}) collective-permute-start(bf16[128,8,128]{2,1,0:T(8,128)(2,1)} %get-tuple-element.33), channel_id=1, source_target_pairs={{0,16},{16,0},{32,48},{48,32},{64,80},{80,64},{96,112},{112,96},{1... | collective-permute-start | bytes 786440 | tf_op jit(solution)/shard_map/ppermute | solution.py:375
  25.9 14.7 %collective-permute-start.7 = (bf16[512,256]{1,0:T(8,128)(2,1)S(1)}, bf16[512,256]{1,0:T(8,128)(2,1)S(1)}, u32[]{:S(2)}, u32[]{:S(2)}) collective-permute-start(bf16[512,256]{1,0:T(8,128)(2,1)S(1)} %pad_maximum_fusion.1.rest_0_), channel_id=1, source_target_pairs={{0,192},{16,208},{32,224},{48,240},{64,128},{80,144},{96,160},{112... | collective-permute-start | bytes 786440 | tf_op jit(solution)/shard_map/ppermute | solution.py:382
  29.0 12.3 %collective-permute-start.6 = (bf16[512,256]{1,0:T(8,128)(2,1)S(1)}, bf16[512,256]{1,0:T(8,128)(2,1)S(1)}, u32[]{:S(2)}, u32[]{:S(2)}) collective-permute-start(bf16[512,256]{1,0:T(8,128)(2,1)S(1)} %pad_maximum_fusion.1.rest_0_), channel_id=1, source_target_pairs={{0,128},{16,144},{32,160},{48,176},{64,192},{80,208},{96,224},{112... | collective-permute-start | bytes 786440 | tf_op jit(solution)/shard_map/ppermute | solution.py:382
  29.6 12.3 %collective-permute-start.5 = (bf16[512,256]{1,0:T(8,128)(2,1)S(1)}, bf16[512,256]{1,0:T(8,128)(2,1)S(1)}, u32[]{:S(2)}, u32[]{:S(2)}) collective-permute-start(bf16[512,256]{1,0:T(8,128)(2,1)S(1)} %pad_maximum_fusion.1.rest_0_), channel_id=1, source_target_pairs={{0,64},{16,80},{32,96},{48,112},{64,0},{80,16},{96,32},{112,48},{1... | collective-permute-start | bytes 786440 | tf_op jit(solution)/shard_map/ppermute | solution.py:382
  31.9 0.7 copy-start.10
  32.6 0.7 copy-start.12
  40.5 0.7 copy-start.14
  41.2 0.7 copy-start.17
  41.9 0.7 copy-start.19
  42.6 1.0 copy-start.11
  43.6 0.9 copy-start.13
  44.5 0.9 copy-start.15
  45.5 0.9 copy-start.18
  46.4 0.9 copy-start.20
  56.2 0.7 copy-start.5
  56.9 0.7 copy-start.16
  58.5 32.5 %collective-permute-start.9 = (bf16[512,256]{1,0:T(8,128)(2,1)}, bf16[512,256]{1,0:T(8,128)(2,1)S(1)}, u32[]{:S(2)}, u32[]{:S(2)}) collective-permute-start(bf16[512,256]{1,0:T(8,128)(2,1)} %get-tuple-element.28), channel_id=1, source_target_pairs={{0,64},{16,80},{32,96},{48,112},{64,0},{80,16},{96,32},{112,48},{1... | collective-permute-start | bytes 786440 | tf_op jit(solution)/shard_map/ppermute | solution.py:382
  58.5 32.5 %collective-permute-start.11 = (bf16[512,256]{1,0:T(8,128)(2,1)}, bf16[512,256]{1,0:T(8,128)(2,1)S(1)}, u32[]{:S(2)}, u32[]{:S(2)}) collective-permute-start(bf16[512,256]{1,0:T(8,128)(2,1)} %get-tuple-element.29), channel_id=1, source_target_pairs={{0,192},{16,208},{32,224},{48,240},{64,128},{80,144},{96,160},{112... | collective-permute-start | bytes 786440 | tf_op jit(solution)/shard_map/ppermute | solution.py:382
  66.7 24.3 %collective-permute-start.10 = (bf16[512,256]{1,0:T(8,128)(2,1)}, bf16[512,256]{1,0:T(8,128)(2,1)S(1)}, u32[]{:S(2)}, u32[]{:S(2)}) collective-permute-start(bf16[512,256]{1,0:T(8,128)(2,1)} %get-tuple-element.30), channel_id=1, source_target_pairs={{0,128},{16,144},{32,160},{48,176},{64,192},{80,208},{96,224},{112... | collective-permute-start | bytes 786440 | tf_op jit(solution)/shard_map/ppermute | solution.py:382
  68.1 23.1 %collective-permute-start.8 = (bf16[2,512,128]{2,1,0:T(8,128)(2,1)}, bf16[2,512,128]{2,1,0:T(8,128)(2,1)S(1)}, u32[]{:S(2)}, u32[]{:S(2)}) collective-permute-start(bf16[2,512,128]{2,1,0:T(8,128)(2,1)} %copy-done.16), channel_id=1, source_target_pairs={{0,16},{16,0},{32,48},{48,32},{64,80},{80,64},{96,112},{112,96},{1... | collective-permute-start | bytes 786440 | tf_op jit(solution)/shard_map/ppermute | solution.py:375
  68.1 1.9 %copy-start = (bf16[1,2048,768]{2,1,0:T(8,128)(2,1)S(1)}, bf16[1,2048,768]{2,1,0:T(8,128)(2,1)}, u32[]{:S(2)}) copy-start(bf16[1,2048,768]{2,1,0:T(8,128)(2,1)} %rest_0_.1) | copy-start | bytes 9437188
  70.0 1.9 %copy-start.1 = (bf16[1,2048,768]{2,1,0:T(8,128)(2,1)S(1)}, bf16[1,2048,768]{2,1,0:T(8,128)(2,1)}, u32[]{:S(2)}) copy-start(bf16[1,2048,768]{2,1,0:T(8,128)(2,1)} %rest_1_.1) | copy-start | bytes 9437188
  71.9 1.9 %copy-start.2 = (bf16[1,768,2048]{2,1,0:T(8,128)(2,1)S(1)}, bf16[1,768,2048]{2,1,0:T(8,128)(2,1)}, u32[]{:S(2)}) copy-start(bf16[1,768,2048]{2,1,0:T(8,128)(2,1)} %rest_2_.1) | copy-start | bytes 9437188
  82.7 8.6 %copy-start.6 = (bf16[2,512,128]{2,1,0:T(8,128)(2,1)S(1)}, bf16[2,512,128]{2,1,0:T(8,128)(2,1)}, u32[]{:S(2)}) copy-start(bf16[2,512,128]{2,1,0:T(8,128)(2,1)} %copy-done.5) | copy-start | bytes 786436
  82.7 29.5 %all-to-all-start.1 = ((bf16[16,160,128]{2,1,0:T(8,128)(2,1)}), bf16[16,160,128]{2,1,0:T(8,128)(2,1)S(1)}, u32[]{:S(2)}, u32[]{:S(2)}) async-start(bf16[16,160,128]{2,1,0:T(8,128)(2,1)} %experts.1), calls=%async_computation.1 | async-start | bytes 1310720 | tf_op jit(solution)/shard_map/all_to_all | solution.py:403
  91.2 7.6 %collective-permute-start.12 = (bf16[256,256]{1,0:T(8,128)(2,1)S(1)}, bf16[256,256]{1,0:T(8,128)(2,1)S(1)}, u32[]{:S(2)}, u32[]{:S(2)}) collective-permute-start(bf16[256,256]{1,0:T(8,128)(2,1)S(1)} %slice.130), channel_id=1, source_target_pairs={{0,32},{16,48},{32,0},{48,16},{64,96},{80,112},{96,64},{112,80},{1... | collective-permute-start | bytes 393224 | tf_op jit(solution)/shard_map/ppermute | solution.py:381
  98.9 1.3 %collective-permute-start.13 = (bf16[128,256]{1,0:T(8,128)(2,1)S(1)}, bf16[128,256]{1,0:T(8,128)(2,1)S(1)}, u32[]{:S(2)}, u32[]{:S(2)}) collective-permute-start(bf16[128,256]{1,0:T(8,128)(2,1)S(1)} %broadcast_select_fusion.7), channel_id=1, source_target_pairs={{0,16},{16,0},{32,48},{48,32},{64,80},{80,64},{96,112},{112,96},{1... | collective-permute-start | bytes 196616 | tf_op jit(solution)/shard_map/ppermute | solution.py:375

commit v3 on v2

--- a/solution.py
+++ b/solution.py
@@ -11,6 +11,7 @@
 SLOT = 10
 LANES = 128
 CHUNK = 256
+MIB = 1024 * 1024
 VMEM = pl.BlockSpec(memory_space=pltpu.VMEM)
 SMEM = pl.BlockSpec(memory_space=pltpu.SMEM)
 ANY = pl.BlockSpec(memory_space=pl.ANY)
@@ -30,11 +31,17 @@
     return lax.dot_general(left, right, (((0,), (0,)), ((), ())), preferred_element_type=F32)
 
 
+def split3(array):
+    high = array.astype(BF16)
+    rest = array - high.astype(F32)
+    middle = rest.astype(BF16)
+    return high, middle, (rest - middle.astype(F32)).astype(BF16)
+
+
 def attention_kernel(
     scale,
     kv_blocks,
     span_ref,
-    chip_ref,
     q_own,
     q_got,
     d_own,
@@ -44,10 +51,12 @@
     *rest,
 ):
     kv_refs = rest[:kv_blocks]
-    dq_own, dq_got, own_ref, part_ref = rest[kv_blocks : kv_blocks + 4]
-    keys, values, keys_t, dk_acc, dv_acc, dq_acc = rest[kv_blocks + 4 :]
-    chip = chip_ref[0]
-    core = chip_ref[1]
+    dq_own, dq_got, own_ref = rest[kv_blocks : kv_blocks + 3]
+    part_refs = rest[kv_blocks + 3 : 2 * kv_blocks + 2]
+    keys, values, keys_t, dk_acc, dv_acc, dq_acc, stat_acc = rest[2 * kv_blocks + 2 :]
+    me = lax.axis_index("ctx")
+    chip = me // 2
+    core = me % 2
     slots = span_ref.shape[0]
     half = keys.shape[0] // slots
     width = q_own.shape[1]
@@ -56,6 +65,21 @@
     def span_of(chip_index, core_index, upper):
         place = chip_index * 2 + core_index
         return span_ref[slots - 1 - place if upper else place]
+
+    stats = jnp.concatenate([stat_own[...], stat_got[...]], axis=0)
+    rows = stats.shape[1]
+    wide = rows * repeat
+    spread = (
+        lax.broadcasted_iota(jnp.int32, (rows, wide), 1) // repeat
+        == lax.broadcasted_iota(jnp.int32, (rows, wide), 0)
+    ).astype(F32).astype(BF16)
+    high, middle, low = split3(stats)
+    lanes = dot(high, spread) + (dot(middle, spread) + dot(low, spread))
+    count = stats.shape[0] // repeat
+    lanes = lanes.reshape(count, repeat, wide)
+    head = lax.broadcasted_iota(jnp.int32, lanes.shape, 1)
+    lane_head = lax.broadcasted_iota(jnp.int32, lanes.shape, 2) % repeat
+    stat_acc[...] = jnp.sum(jnp.where(head == lane_head, lanes, 0.0), axis=1)
 
     for block in range(kv_blocks):
         for part in range(8):
@@ -76,14 +100,15 @@
     for index in range(4):
         upper = index % 2
         if index < 2:
-            q_ref, d_ref, stat_ref, dq_ref, who = q_own, d_own, stat_own, dq_own, core
+            q_ref, d_ref, dq_ref, who = q_own, d_own, dq_own, core
         else:
-            q_ref, d_ref, stat_ref, dq_ref, who = q_got, d_got, stat_got, dq_got, 1 - core
+            q_ref, d_ref, dq_ref, who = q_got, d_got, dq_got, 1 - core
+        line = 2 * (index // 2)
         span = span_of(chip, who, upper)
         queries = q_ref[upper]
         grads = d_ref[upper]
-        norm = stat_ref[0:1, upper * width : (upper + 1) * width] * (1.0 / math.log(2.0))
-        inner = stat_ref[1:2, upper * width : (upper + 1) * width]
+        norm = stat_acc[line : line + 1, upper * width : (upper + 1) * width] * (1.0 / math.log(2.0))
+        inner = stat_acc[line + 1 : line + 2, upper * width : (upper + 1) * width]
         dq_acc[...] = jnp.zeros_like(dq_acc)
         last = span // spans_in_chunk
 
@@ -115,25 +140,26 @@
                 own_ref[rows, :LANES] = dk_acc[at, :] * scale
                 own_ref[rows, LANES:] = dv_acc[at, :]
             else:
-                part_ref[block - 1, rows, :LANES] = (dk_acc[at, :] * scale).astype(BF16)
-                part_ref[block - 1, rows, LANES:] = dv_acc[at, :].astype(BF16)
-
-
-def attention(span_order, place, q_own, q_got, d_own, d_got, stat_own, stat_got, kv_list, scale):
+                part_refs[block - 1][rows, :LANES] = (dk_acc[at, :] * scale).astype(BF16)
+                part_refs[block - 1][rows, LANES:] = dv_acc[at, :].astype(BF16)
+
+
+def attention(span_order, q_own, q_got, d_own, d_got, stat_own, stat_got, kv_list, scale):
     blocks = len(kv_list)
     rows = kv_list[0].shape[0]
     total = blocks * rows
     spans, width, _ = q_own.shape
+    part = jax.ShapeDtypeStruct((rows, 2 * LANES), BF16)
     return pl.pallas_call(
         functools.partial(attention_kernel, scale, blocks),
         out_shape=(
             jax.ShapeDtypeStruct(q_own.shape, BF16),
             jax.ShapeDtypeStruct(q_own.shape, BF16),
             jax.ShapeDtypeStruct((rows, 2 * LANES), F32),
-            jax.ShapeDtypeStruct((blocks - 1, rows, 2 * LANES), BF16),
-        ),
-        in_specs=[SMEM, SMEM] + [VMEM] * (6 + blocks),
-        out_specs=(VMEM,) * 4,
+        )
+        + (part,) * (blocks - 1),
+        in_specs=[SMEM] + [VMEM] * (6 + blocks),
+        out_specs=(VMEM,) * (2 + blocks),
         scratch_shapes=[
             pltpu.VMEM((total, LANES), BF16),
             pltpu.VMEM((total, LANES), BF16),
@@ -141,15 +167,16 @@
             pltpu.VMEM((total, LANES), F32),
             pltpu.VMEM((total, LANES), F32),
             pltpu.VMEM((LANES, width), F32),
+            pltpu.VMEM((4, spans * width), F32),
         ],
-        compiler_params=pltpu.CompilerParams(vmem_limit_bytes=16 * 1024 * 1024),
+        compiler_params=pltpu.CompilerParams(vmem_limit_bytes=16 * MIB),
         cost_estimate=pl.CostEstimate(
             flops=6 * spans * width * total * LANES * 2,
             bytes_accessed=6 * 1024 * 1024,
             transcendentals=spans * width * total,
         ),
         name="attention",
-    )(span_order, place, q_own, q_got, d_own, d_got, stat_own, stat_got, *kv_list)
+    )(span_order, q_own, q_got, d_own, d_got, stat_own, stat_got, *kv_list)
 
 
 def slots_to_chunks(tiles, experts, blocks, chunk_ref, first):
@@ -218,7 +245,7 @@
             pltpu.VMEM((experts, 2 * blocks * SLOT, LANES), F32),
             pltpu.SemaphoreType.DMA((2,)),
         ],
-        compiler_params=pltpu.CompilerParams(vmem_limit_bytes=12 * 1024 * 1024),
+        compiler_params=pltpu.CompilerParams(vmem_limit_bytes=60 * MIB),
         name="dispatch",
     )(ids.T, keep.T, weight.T, x, g)
 
@@ -287,7 +314,7 @@
             pltpu.VMEM((slots, width), BF16),
             pltpu.SemaphoreType.DMA((9,)),
         ],
-        compiler_params=pltpu.CompilerParams(vmem_limit_bytes=28 * 1024 * 1024),
+        compiler_params=pltpu.CompilerParams(vmem_limit_bytes=58 * MIB),
         cost_estimate=pl.CostEstimate(
             flops=10 * slots * width * hidden, bytes_accessed=11 * 1024 * 1024, transcendentals=slots * hidden
         ),
@@ -327,7 +354,7 @@
             pltpu.VMEM((experts, chunk_rows, LANES), F32),
             pltpu.VMEM((blocks, slots, LANES), F32),
         ],
-        compiler_params=pltpu.CompilerParams(vmem_limit_bytes=12 * 1024 * 1024),
+        compiler_params=pltpu.CompilerParams(vmem_limit_bytes=12 * MIB),
         name="combine",
     )(weight, back)
 
@@ -354,63 +381,58 @@
     scale = 1.0 / math.sqrt(size)
     members = lax.axis_size("ctx")
     experts = lax.axis_size("exp")
-    me = lax.axis_index("ctx")
-    core = me % 2
-    first = core == 0
+    first = lax.axis_index("ctx") & 1 == 0
     chips = members // 2
-    swap = [(i, i ^ 1) for i in range(members)]
-
-    send, weight = dispatch(expert_ids, keep_mask, route_weight, moe_input, moe_grad, experts)
-
-    def halves(array):
-        low, high = array[:, :group], array[:, group:]
-        return jnp.where(first, low, high), jnp.where(first, high, low)
-
-    q_own, q_away = halves(queries)
-    d_own, d_away = halves(out_grad)
-    stat_own, stat_away = halves(jnp.stack([log_norm, out_dot]).reshape(2 * rows, heads))
+    trade = lambda array, k: lax.ppermute(array, "ctx", [(i, i ^ k) for i in range(members)])
+
     kv = jnp.concatenate([key_tensor, value_tensor], axis=2)
     kv_own = jnp.where(first, kv[:, 0], kv[:, 1])
     kv_away = jnp.where(first, kv[:, 1], kv[:, 0])
-    trade = lambda array: lax.ppermute(array, "ctx", swap)
-    kv_got = trade(kv_away)
-    q_got, d_got = trade(q_away), trade(d_away)
-    stat_got = trade(stat_away.reshape(2, rows * group))
-    kv_chip = jnp.concatenate([jnp.where(first, kv_own, kv_got), jnp.where(first, kv_got, kv_own)], axis=0)
-
-    neighbour = lambda array: lax.ppermute(array, "ctx", [(i, i ^ 2) for i in range(members)])
-    along_y = lambda array, k: lax.ppermute(array, "ctx", [(i, i ^ (4 * k)) for i in range(members)])
-    kv_pair = jnp.concatenate([kv_chip, neighbour(kv_chip)], axis=0)
+    kv_own, kv_away, expert_ids = lax.optimization_barrier((kv_own, kv_away, expert_ids))
+    kv_got = trade(kv_away, 1)
+    kv_near, kv_cross = trade(kv_own, 2), trade(kv_away, 3)
+    send, weight = dispatch(expert_ids, keep_mask, route_weight, moe_input, moe_grad, experts)
+    ordered = lambda mine, other: [jnp.where(first, mine, other), jnp.where(first, other, mine)]
+    kv_pair = jnp.concatenate(ordered(kv_own, kv_got) + ordered(kv_near, kv_cross), axis=0)
+    send, kv_pair = lax.optimization_barrier((send, kv_pair))
     received = lax.all_to_all(send, "exp", split_axis=0, concat_axis=0, tiled=True)
-    kv_list = [kv_pair] + [along_y(kv_pair, k) for k in range(1, chips // 2)]
+    kv_list = [kv_pair] + [trade(kv_pair, 4 * k) for k in range(1, chips // 2)]
+
+    def halves(array, axis):
+        low, high = jnp.split(array, 2, axis=axis)
+        return jnp.where(first, low, high), jnp.where(first, high, low)
+
+    q_own, q_away = halves(queries, 1)
+    d_own, d_away = halves(out_grad, 1)
+    stat_own, stat_away = halves(jnp.stack([log_norm.T, out_dot.T]), 1)
+    q_got, d_got = trade(q_away, 1), trade(d_away, 1)
+    stat_got = trade(stat_away, 1)
 
     spans = lambda array: array.reshape(2, rows // 2 * group, size)
-    place = jnp.stack([me // 2, core]).astype(jnp.int32)
-    dq_own, dq_got, own_sum, parts = attention(
+    dq_own, dq_got, own_sum, *parts = attention(
         span_order,
-        place,
         spans(q_own),
         spans(q_got),
         spans(d_own),
         spans(d_got),
-        stat_own.reshape(2, rows * group),
-        stat_got,
+        stat_own.reshape(2 * group, rows),
+        stat_got.reshape(2 * group, rows),
         kv_list,
         scale,
     )
-    received, parts = lax.optimization_barrier((received, parts))
+    received, *parts = lax.optimization_barrier((received, *parts))
     slot_grad = mlp(received, w_gate, w_up, w_down)
     returned = lax.all_to_all(slot_grad, "exp", split_axis=0, concat_axis=0, tiled=True)
 
     total = own_sum
     for k in range(1, chips // 2):
-        total = total + along_y(parts[k - 1], k).astype(F32)
-    total = total[: 2 * rows] + neighbour(total[2 * rows :].astype(BF16)).astype(F32)
+        total = total + trade(parts[k - 1], 4 * k).astype(F32)
+    total = total[: 2 * rows] + trade(total[2 * rows :].astype(BF16), 2).astype(F32)
     total = total.astype(BF16)
     low, high = total[:rows], total[rows:]
     kv_mine = jnp.where(first, low, high)
-    kv_theirs = trade(jnp.where(first, high, low))
-    dq_back = trade(dq_got)
+    kv_theirs = trade(jnp.where(first, high, low), 1)
+    dq_back = trade(dq_got, 1)
 
     def joined(mine, theirs):
         return jnp.concatenate([jnp.where(first, mine, theirs), jnp.where(first, theirs, mine)], axis=1)

time: 114 us -> 96.3 us (0.84)
  local copies, waits for them, and re-layouts: 23.9 us -> 3.27 us
  starting transfers between devices: 33.1 us -> 26.5 us
  Pallas kernels: 21.5 us -> 26.6 us
  waiting for transfers between devices: 31.5 us -> 36 us
    unnamed x59 -> x15, local copies, waits for them, and re-layouts: 20.9 us -> 2.34 us
    all_to_all x1, waiting for transfers between devices: 0.01 us -> 6.33 us  [on_device(): lax.all_to_all(send, 'exp', split_axis=0, concat_axis=0, tiled=True)]
    all_to_all x1, starting transfers between devices: 8.26 us -> 3.6 us  [on_device(): lax.all_to_all(slot_grad, 'exp', split_axis=0, concat_axis=0, tiled=True)]
    pallas_call x1, Pallas kernels: 8.78 us -> 10.7 us  [attention(): pl.pallas_call(functools.partial(attention_kernel, scale, blocks), out_sh...]
    ppermute x14 -> x15, waiting for transfers between devices: 20.9 us -> 19.1 us  [on_device(): lax.ppermute(array, 'ctx', [(i, i ^ k) for i in range(members)])]
    pallas_call x1, Pallas kernels: 8.86 us -> 10.6 us  [mlp(): pl.pallas_call(mlp_kernel, out_shape=jax.ShapeDtypeStruct((sources, block...]
    pallas_call x1, Pallas kernels: 2.34 us -> 3.8 us  [dispatch(): pl.pallas_call(dispatch_kernel, out_shape=(jax.ShapeDtypeStruct((experts,...]
    ppermute x14 -> x15, starting transfers between devices: 15.6 us -> 14.2 us  [on_device(): lax.ppermute(array, 'ctx', [(i, i ^ k) for i in range(members)])]
  transfers between devices with their start and end apart: 16 -> 17, of which waited for: 6 -> 7; matrix products, arithmetic and copies ran while one was open for 6% -> 4% of each run, Pallas kernels for 16% -> 26%
where the time goes in v3:
time: 96.3 us; the launch traced here: 95.6 us
  waiting for transfers between devices  36 us (37%)
  Pallas kernels  26.6 us (28%)
  starting transfers between devices  26.5 us (28%)
  local copies, waits for them, and re-layouts  3.27 us (3%)
  other arithmetic  2.21 us (2%)
    ppermute x15, waiting for transfers between devices, on_device(): lax.ppermute(array, 'ctx', [(i, i ^ k) for i in range(members)])  19.1 us
    ppermute x15, starting transfers between devices, on_device(): lax.ppermute(array, 'ctx', [(i, i ^ k) for i in range(members)])  14.2 us
    pallas_call x1, Pallas kernels, attention(): pl.pallas_call(functools.partial(attention_kernel, scale, blocks), out_sh...  10.7 us
    pallas_call x1, Pallas kernels, mlp(): pl.pallas_call(mlp_kernel, out_shape=jax.ShapeDtypeStruct((sources, block...  10.6 us
    all_to_all x1, waiting for transfers between devices, on_device(): lax.all_to_all(slot_grad, 'exp', split_axis=0, concat_axis=0, tiled=True)  10.6 us
    all_to_all x1, starting transfers between devices, on_device(): lax.all_to_all(send, 'exp', split_axis=0, concat_axis=0, tiled=True)  8.66 us
    all_to_all x1, waiting for transfers between devices, on_device(): lax.all_to_all(send, 'exp', split_axis=0, concat_axis=0, tiled=True)  6.33 us
    pallas_call x1, Pallas kernels, dispatch(): pl.pallas_call(dispatch_kernel, out_shape=(jax.ShapeDtypeStruct((experts,...  3.8 us
  transfers between devices with their start and end apart: 17, of which 7 were waited for; matrix products, arithmetic and copies ran while one was open for 4% of the time, Pallas kernels for 26%

profile of v3, /device:TPU:4, one launch (start us, length us, event | category | flops | bytes accessed | tf_op | source)
XLA Modules:
  0.0 95.6 jit_solution(12544413619828300899)
XLA Ops:
  0.6 0.0 copy-start.4
  0.6 0.0 copy-start.5
  0.7 0.0 copy-start.2
  0.7 0.9 copy_dynamic-update-slice_fusion.1
  1.6 0.0 copy-start.3
  1.6 0.9 copy_dynamic-update-slice_fusion
  2.5 0.1 collective-permute-start.3
  2.6 2.4 %collective-permute-start.5 = (bf16[128,256]{1,0:T(8,128)(2,1)S(1)}, bf16[128,256]{1,0:T(8,128)(2,1)S(1)}, u32[]{:S(2)}, u32[]{:S(2)}) collective-permute-start(bf16[128,256]{1,0:T(8,128)(2,1)S(1)} %get-tuple-element.24), channel_id=1, source_target_pairs={{0,48},{16,32},{32,16},{48,0},{64,112},{80,96},{96,80},{112,64},{1... | collective-permute-start | bytes 196616 | tf_op jit(solution)/shard_map/ppermute | solution.py:386
  5.0 1.3 %collective-permute-start.4 = (bf16[128,256]{1,0:T(8,128)(2,1)S(1)}, bf16[128,256]{1,0:T(8,128)(2,1)S(1)}, u32[]{:S(2)}, u32[]{:S(2)}) collective-permute-start(bf16[128,256]{1,0:T(8,128)(2,1)S(1)} %get-tuple-element.23), channel_id=1, source_target_pairs={{0,32},{16,48},{32,0},{48,16},{64,96},{80,112},{96,64},{112,80},{1... | collective-permute-start | bytes 196616 | tf_op jit(solution)/shard_map/ppermute | solution.py:386
  6.3 3.8 %dispatch.1 = (bf16[16,320,128]{2,1,0:T(8,128)(2,1)}, f32[160,128]{1,0:T(8,128)}) custom-call(s32[8,128]{1,0:T(8,128)} %bitcast.35, s32[8,128]{1,0:T(8,128)} %bitcast.36, f32[8,128]{1,0:T(8,128)} %bitcast.37, bf16[128,2048]{1,0:T(8,128)(2,1)} %x_hbm.1, bf16[128,2048]{1,0:T(8,128)(2,1)} %g_hbm.1), custom_call_target="tpu_custom_call" | custom-call | tf_op jit(solution)/shard_map/dispatch/pallas_call | solution.py:233
  10.1 0.0 copy-start.1
  10.1 0.0 collective-permute-done.3
  10.1 0.6 collective-permute-done.4
  10.8 0.0 collective-permute-done.5
  10.8 8.7 %all-to-all-start = ((bf16[16,320,128]{2,1,0:T(8,128)(2,1)}), bf16[16,320,128]{2,1,0:T(8,128)(2,1)}, u32[]{:S(2)}, u32[]{:S(2)}) async-start(bf16[16,320,128]{2,1,0:T(8,128)(2,1)} %get-tuple-element.29), calls=%async_computation | async-start | bytes 2621440 | tf_op jit(solution)/shard_map/all_to_all | solution.py:398
  19.5 0.0 copy-done.4
  19.5 0.0 copy-done.5
  19.5 0.1 collective-permute-start.2
  19.6 0.0 copy-done.2
  19.7 0.6 collective-permute-start
  20.3 0.0 copy-done.3
  20.3 0.1 collective-permute-start.1
  20.4 3.1 %collective-permute-start.8 = (bf16[512,256]{1,0:T(8,128)(2,1)S(1)}, bf16[512,256]{1,0:T(8,128)(2,1)S(1)}, u32[]{:S(2)}, u32[]{:S(2)}) collective-permute-start(bf16[512,256]{1,0:T(8,128)(2,1)S(1)} %pad_maximum_fusion.1.rest_0_), channel_id=1, source_target_pairs={{0,192},{16,208},{32,224},{48,240},{64,128},{80,144},{96,160},{112... | collective-permute-start | bytes 786440 | tf_op jit(solution)/shard_map/ppermute | solution.py:386
  23.5 0.6 collective-permute-start.7
  24.1 0.0 collective-permute-done.2
  24.1 0.5 collective-permute-start.6
  24.6 0.0 collective-permute-done
  24.6 0.0 collective-permute-done.1
  24.6 11.4 %collective-permute-done.8.rest_3_ = bf16[512,256]{1,0:T(8,128)(2,1)S(1)} collective-permute-done((bf16[512,256]{1,0:T(8,128)(2,1)S(1)}, bf16[512,256]{1,0:T(8,128)(2,1)S(1)}, u32[]{:S(2)}, u32[]{:S(2)}) %collective-permute-start.8) | collective-permute-done | bytes 262176 | tf_op jit(solution)/shard_map/ppermute | solution.py:386
  36.0 0.0 collective-permute-done.7.rest_2_
  36.0 0.6 collective-permute-done.6.rest_1_
  36.6 0.0 copy-done.1
  36.6 10.7 %attention.1 = (bf16[2,512,128]{2,1,0:T(8,128)(2,1)S(1)}, bf16[2,512,128]{2,1,0:T(8,128)(2,1)S(1)}, f32[512,256]{1,0:T(8,128)S(1)}, bf16[512,256]{1,0:T(8,128)(2...) custom-call(s32[32]{0:T(128)S(1)} %copy-done.1, bf16[2,512,128]{2,1,0:T(8,128)(2,1)S(1)} %bitcast.26, ...), custom_call_target="tpu_custom_call" | custom-call | flops 3221225472 | bytes 6291456 | tf_op jit(solution)/shard_map/attention/pallas_call | solution.py:153
  47.3 6.3 %all-to-all-done.in_ref = bf16[16,320,128]{2,1,0:T(8,128)(2,1)} async-done(((bf16[16,320,128]{2,1,0:T(8,128)(2,1)}), bf16[16,320,128]{2,1,0:T(8,128)(2,1)}, u32[]{:S(2)}, u32[]{:S(2)}) %all-to-all-start) | async-done | bytes 1310752 | tf_op jit(solution)/shard_map/all_to_all | solution.py:398
  53.7 1.6 %collective-permute-start.10 = (bf16[512,256]{1,0:T(8,128)(2,1)S(1)}, bf16[512,256]{1,0:T(8,128)(2,1)S(1)}, u32[]{:S(2)}, u32[]{:S(2)}) collective-permute-start(bf16[512,256]{1,0:T(8,128)(2,1)S(1)} %get-tuple-element.33), channel_id=1, source_target_pairs={{0,64},{16,80},{32,96},{48,112},{64,0},{80,16},{96,32},{112,48},{1... | collective-permute-start | bytes 786440 | tf_op jit(solution)/shard_map/ppermute | solution.py:386
  55.2 2.9 %collective-permute-start.11 = (bf16[512,256]{1,0:T(8,128)(2,1)S(1)}, bf16[512,256]{1,0:T(8,128)(2,1)S(1)}, u32[]{:S(2)}, u32[]{:S(2)}) collective-permute-start(bf16[512,256]{1,0:T(8,128)(2,1)S(1)} %get-tuple-element.34), channel_id=1, source_target_pairs={{0,128},{16,144},{32,160},{48,176},{64,192},{80,208},{96,224},{112... | collective-permute-start | bytes 786440 | tf_op jit(solution)/shard_map/ppermute | solution.py:386
  58.1 0.2 collective-permute-start.12
  58.4 0.0 collective-permute-start.9
  58.4 10.6 %experts.1 = bf16[16,160,128]{2,1,0:T(8,128)(2,1)} custom-call(bf16[16,320,128]{2,1,0:T(8,128)(2,1)} %all-to-all-done.in_ref, bf16[1,2048,768]{2,1,0:T(8,128)(2,1)} %rest_0_.1, bf16[1,2048,768]{2,1,0:T(8,128)(2,1)} %rest_1_.1, bf16[1,768,2048]{2,1,0:T(8,128)(2,1)} %rest_2_.1), custom_call_target="tpu_custom_call" | custom-call | flops 2516582400 | bytes 11534336 | tf_op jit(solution)/shard_map/experts/pallas_call | solution.py:302
  69.0 3.6 %all-to-all-start.1 = ((bf16[16,160,128]{2,1,0:T(8,128)(2,1)}), bf16[16,160,128]{2,1,0:T(8,128)(2,1)S(1)}, u32[]{:S(2)}, u32[]{:S(2)}) async-start(bf16[16,160,128]{2,1,0:T(8,128)(2,1)} %experts.1), calls=%async_computation.1 | async-start | bytes 1310720 | tf_op jit(solution)/shard_map/all_to_all | solution.py:425
  72.6 0.0 copy-start
  72.6 0.0 collective-permute-done.10
  72.6 0.0 collective-permute-done.11
  72.7 0.0 collective-permute-done.12
  72.7 0.1 convert_add_fusion
  72.8 0.8 collective-permute-start.13
  73.6 0.0 collective-permute-done.9
  73.6 1.0 %broadcast_select_fusion.5 = (bf16[2,512,128]{2,1,0:T(8,128)(2,1)S(1)}, bf16[2,512,128]{2,1,0:T(8,128)(2,1)S(1)}) fusion(bf16[2,512,128]{2,1,0:T(8,128)(2,1)S(1)} %get-tuple-element.26, bf16[2,512,128]{2,1,0:T(8,128)(2,1)} %collective-permute-done.9, pred[]{:T(512)S(6)} %eq.3), kind=kLoop, calls=%fused_computation.11 | loop fusion | flops 262144 | bytes 1048577 | tf_op jit(solution)/shard_map/jit(_where)/select_n | solution.py:438
  74.6 6.0 %collective-permute-done.13 = bf16[256,256]{1,0:T(8,128)(2,1)S(1)} collective-permute-done((bf16[256,256]{1,0:T(8,128)(2,1)S(1)}, bf16[256,256]{1,0:T(8,128)(2,1)S(1)}, u32[]{:S(2)}, u32[]{:S(2)}) %collective-permute-start.13) | collective-permute-done | bytes 131104 | tf_op jit(solution)/shard_map/ppermute | solution.py:386
  80.7 0.1 collective-permute-start.14
  80.8 0.9 pad_maximum_fusion
  81.6 0.4 collective-permute-done.14
  82.1 0.7 copy.22
  82.8 0.7 copy.21
  83.4 10.6 %all-to-all-done.1.back_ref = bf16[16,160,128]{2,1,0:T(8,128)(2,1)S(1)} async-done(((bf16[16,160,128]{2,1,0:T(8,128)(2,1)}), bf16[16,160,128]{2,1,0:T(8,128)(2,1)S(1)}, u32[]{:S(2)}, u32[]{:S(2)}) %all-to-all-start.1) | async-done | bytes 655392 | tf_op jit(solution)/shard_map/all_to_all | solution.py:425
  94.1 0.0 copy-done
  94.1 1.5 %combine.1 = bf16[128,2048]{1,0:T(8,128)(2,1)} custom-call(f32[160,128]{1,0:T(8,128)S(1)} %copy-done, bf16[16,160,128]{2,1,0:T(8,128)(2,1)S(1)} %all-to-all-done.1.back_ref), custom_call_target="tpu_custom_call" | custom-call | tf_op jit(solution)/shard_map/combine/pallas_call | solution.py:348
  (12 shorter events, 0.2 us)
Async XLA Ops:
  0.6 18.9 %copy-start.4 = (f32[128,16]{0,1:T(8,128)S(1)}, f32[128,16]{0,1:T(8,128)}, u32[]{:S(2)}) copy-start(f32[128,16]{0,1:T(8,128)} %param.20) | copy-start | bytes 24580
  0.6 18.9 %copy-start.5 = (f32[128,16]{0,1:T(8,128)S(1)}, f32[128,16]{0,1:T(8,128)}, u32[]{:S(2)}) copy-start(f32[128,16]{0,1:T(8,128)} %param.19) | copy-start | bytes 24580
  0.7 19.0 %copy-start.2 = (bf16[128,16,128]{2,1,0:T(8,128)(2,1)S(1)}, bf16[128,16,128]{2,1,0:T(8,128)(2,1)}, u32[]{:S(2)}) copy-start(bf16[128,16,128]{2,1,0:T(8,128)(2,1)} %param.15) | copy-start | bytes 1572868
  1.6 18.7 %copy-start.3 = (bf16[128,16,128]{2,1,0:T(8,128)(2,1)S(1)}, bf16[128,16,128]{2,1,0:T(8,128)(2,1)}, u32[]{:S(2)}) copy-start(bf16[128,16,128]{2,1,0:T(8,128)(2,1)} %param.18) | copy-start | bytes 1572868
  2.5 7.6 %collective-permute-start.3 = (bf16[128,256]{1,0:T(8,128)(2,1)S(1)}, bf16[128,256]{1,0:T(8,128)(2,1)S(1)}, u32[]{:S(2)}, u32[]{:S(2)}) collective-permute-start(bf16[128,256]{1,0:T(8,128)(2,1)S(1)} %get-tuple-element.24), channel_id=1, source_target_pairs={{0,16},{16,0},{32,48},{48,32},{64,80},{80,64},{96,112},{112,96},{1... | collective-permute-start | bytes 196616 | tf_op jit(solution)/shard_map/ppermute | solution.py:386
  2.6 8.1 %collective-permute-start.5 = (bf16[128,256]{1,0:T(8,128)(2,1)S(1)}, bf16[128,256]{1,0:T(8,128)(2,1)S(1)}, u32[]{:S(2)}, u32[]{:S(2)}) collective-permute-start(bf16[128,256]{1,0:T(8,128)(2,1)S(1)} %get-tuple-element.24), channel_id=1, source_target_pairs={{0,48},{16,32},{32,16},{48,0},{64,112},{80,96},{96,80},{112,64},{1... | collective-permute-start | bytes 196616 | tf_op jit(solution)/shard_map/ppermute | solution.py:386
  5.0 5.8 %collective-permute-start.4 = (bf16[128,256]{1,0:T(8,128)(2,1)S(1)}, bf16[128,256]{1,0:T(8,128)(2,1)S(1)}, u32[]{:S(2)}, u32[]{:S(2)}) collective-permute-start(bf16[128,256]{1,0:T(8,128)(2,1)S(1)} %get-tuple-element.23), channel_id=1, source_target_pairs={{0,32},{16,48},{32,0},{48,16},{64,96},{80,112},{96,64},{112,80},{1... | collective-permute-start | bytes 196616 | tf_op jit(solution)/shard_map/ppermute | solution.py:386
  10.1 26.5 %copy-start.1 = (s32[32]{0:T(128)S(1)}, s32[32]{0:T(128)}, u32[]{:S(2)}) copy-start(s32[32]{0:T(128)} %span_ref.1) | copy-start | bytes 388
  10.8 42.8 %all-to-all-start = ((bf16[16,320,128]{2,1,0:T(8,128)(2,1)}), bf16[16,320,128]{2,1,0:T(8,128)(2,1)}, u32[]{:S(2)}, u32[]{:S(2)}) async-start(bf16[16,320,128]{2,1,0:T(8,128)(2,1)} %get-tuple-element.29), calls=%async_computation | async-start | bytes 2621440 | tf_op jit(solution)/shard_map/all_to_all | solution.py:398
  19.5 4.6 %collective-permute-start.2 = (f32[2,8,128]{2,1,0:T(8,128)S(1)}, f32[2,8,128]{2,1,0:T(8,128)S(1)}, u32[]{:S(2)}, u32[]{:S(2)}) collective-permute-start(f32[2,8,128]{2,1,0:T(8,128)S(1)} %get-tuple-element.58), channel_id=1, source_target_pairs={{0,16},{16,0},{32,48},{48,32},{64,80},{80,64},{96,112},{112,96},{1... | collective-permute-start | bytes 24584 | tf_op jit(solution)/shard_map/ppermute | solution.py:386
  19.7 4.9 %collective-permute-start = (bf16[128,8,128]{2,1,0:T(8,128)(2,1)S(1)}, bf16[128,8,128]{2,1,0:T(8,128)(2,1)S(1)}, u32[]{:S(2)}, u32[]{:S(2)}) collective-permute-start(bf16[128,8,128]{2,1,0:T(8,128)(2,1)S(1)} %get-tuple-element.46), channel_id=1, source_target_pairs={{0,16},{16,0},{32,48},{48,32},{64,80},{80,64},{96,112},{112,96},{1... | collective-permute-start | bytes 786440 | tf_op jit(solution)/shard_map/ppermute | solution.py:386
  20.3 4.3 %collective-permute-start.1 = (bf16[128,8,128]{2,1,0:T(8,128)(2,1)S(1)}, bf16[128,8,128]{2,1,0:T(8,128)(2,1)S(1)}, u32[]{:S(2)}, u32[]{:S(2)}) collective-permute-start(bf16[128,8,128]{2,1,0:T(8,128)(2,1)S(1)} %get-tuple-element.44), channel_id=1, source_target_pairs={{0,16},{16,0},{32,48},{48,32},{64,80},{80,64},{96,112},{112,96},{1... | collective-permute-start | bytes 786440 | tf_op jit(solution)/shard_map/ppermute | solution.py:386
  20.4 15.6 %collective-permute-start.8 = (bf16[512,256]{1,0:T(8,128)(2,1)S(1)}, bf16[512,256]{1,0:T(8,128)(2,1)S(1)}, u32[]{:S(2)}, u32[]{:S(2)}) collective-permute-start(bf16[512,256]{1,0:T(8,128)(2,1)S(1)} %pad_maximum_fusion.1.rest_0_), channel_id=1, source_target_pairs={{0,192},{16,208},{32,224},{48,240},{64,128},{80,144},{96,160},{112... | collective-permute-start | bytes 786440 | tf_op jit(solution)/shard_map/ppermute | solution.py:386
  23.5 12.5 %collective-permute-start.7 = (bf16[512,256]{1,0:T(8,128)(2,1)S(1)}, bf16[512,256]{1,0:T(8,128)(2,1)S(1)}, u32[]{:S(2)}, u32[]{:S(2)}) collective-permute-start(bf16[512,256]{1,0:T(8,128)(2,1)S(1)} %pad_maximum_fusion.1.rest_0_), channel_id=1, source_target_pairs={{0,128},{16,144},{32,160},{48,176},{64,192},{80,208},{96,224},{112... | collective-permute-start | bytes 786440 | tf_op jit(solution)/shard_map/ppermute | solution.py:386
  24.1 12.5 %collective-permute-start.6 = (bf16[512,256]{1,0:T(8,128)(2,1)S(1)}, bf16[512,256]{1,0:T(8,128)(2,1)S(1)}, u32[]{:S(2)}, u32[]{:S(2)}) collective-permute-start(bf16[512,256]{1,0:T(8,128)(2,1)S(1)} %pad_maximum_fusion.1.rest_0_), channel_id=1, source_target_pairs={{0,64},{16,80},{32,96},{48,112},{64,0},{80,16},{96,32},{112,48},{1... | collective-permute-start | bytes 786440 | tf_op jit(solution)/shard_map/ppermute | solution.py:386
  53.7 19.0 %collective-permute-start.10 = (bf16[512,256]{1,0:T(8,128)(2,1)S(1)}, bf16[512,256]{1,0:T(8,128)(2,1)S(1)}, u32[]{:S(2)}, u32[]{:S(2)}) collective-permute-start(bf16[512,256]{1,0:T(8,128)(2,1)S(1)} %get-tuple-element.33), channel_id=1, source_target_pairs={{0,64},{16,80},{32,96},{48,112},{64,0},{80,16},{96,32},{112,48},{1... | collective-permute-start | bytes 786440 | tf_op jit(solution)/shard_map/ppermute | solution.py:386
  55.2 17.4 %collective-permute-start.11 = (bf16[512,256]{1,0:T(8,128)(2,1)S(1)}, bf16[512,256]{1,0:T(8,128)(2,1)S(1)}, u32[]{:S(2)}, u32[]{:S(2)}) collective-permute-start(bf16[512,256]{1,0:T(8,128)(2,1)S(1)} %get-tuple-element.34), channel_id=1, source_target_pairs={{0,128},{16,144},{32,160},{48,176},{64,192},{80,208},{96,224},{112... | collective-permute-start | bytes 786440 | tf_op jit(solution)/shard_map/ppermute | solution.py:386
  58.1 14.5 %collective-permute-start.12 = (bf16[512,256]{1,0:T(8,128)(2,1)S(1)}, bf16[512,256]{1,0:T(8,128)(2,1)S(1)}, u32[]{:S(2)}, u32[]{:S(2)}) collective-permute-start(bf16[512,256]{1,0:T(8,128)(2,1)S(1)} %get-tuple-element.35), channel_id=1, source_target_pairs={{0,192},{16,208},{32,224},{48,240},{64,128},{80,144},{96,160},{112... | collective-permute-start | bytes 786440 | tf_op jit(solution)/shard_map/ppermute | solution.py:386
  58.4 15.2 %collective-permute-start.9 = (bf16[2,512,128]{2,1,0:T(8,128)(2,1)S(1)}, bf16[2,512,128]{2,1,0:T(8,128)(2,1)}, u32[]{:S(2)}, u32[]{:S(2)}) collective-permute-start(bf16[2,512,128]{2,1,0:T(8,128)(2,1)S(1)} %get-tuple-element.27), channel_id=1, source_target_pairs={{0,16},{16,0},{32,48},{48,32},{64,80},{80,64},{96,112},{112,96},{1... | collective-permute-start | bytes 786440 | tf_op jit(solution)/shard_map/ppermute | solution.py:386
  69.0 25.1 %all-to-all-start.1 = ((bf16[16,160,128]{2,1,0:T(8,128)(2,1)}), bf16[16,160,128]{2,1,0:T(8,128)(2,1)S(1)}, u32[]{:S(2)}, u32[]{:S(2)}) async-start(bf16[16,160,128]{2,1,0:T(8,128)(2,1)} %experts.1), calls=%async_computation.1 | async-start | bytes 1310720 | tf_op jit(solution)/shard_map/all_to_all | solution.py:425
  72.6 21.4 %copy-start = (f32[160,128]{1,0:T(8,128)S(1)}, f32[160,128]{1,0:T(8,128)}, u32[]{:S(2)}) copy-start(f32[160,128]{1,0:T(8,128)} %get-tuple-element.36.weight_ref) | copy-start | bytes 245764
  72.8 7.8 %collective-permute-start.13 = (bf16[256,256]{1,0:T(8,128)(2,1)S(1)}, bf16[256,256]{1,0:T(8,128)(2,1)S(1)}, u32[]{:S(2)}, u32[]{:S(2)}) collective-permute-start(bf16[256,256]{1,0:T(8,128)(2,1)S(1)} %slice.69), channel_id=1, source_target_pairs={{0,32},{16,48},{32,0},{48,16},{64,96},{80,112},{96,64},{112,80},{1... | collective-permute-start | bytes 393224 | tf_op jit(solution)/shard_map/ppermute | solution.py:386
  80.7 1.3 %collective-permute-start.14 = (bf16[128,256]{1,0:T(8,128)(2,1)S(1)}, bf16[128,256]{1,0:T(8,128)(2,1)S(1)}, u32[]{:S(2)}, u32[]{:S(2)}) collective-permute-start(bf16[128,256]{1,0:T(8,128)(2,1)S(1)} %broadcast_select_fusion.6), channel_id=1, source_target_pairs={{0,16},{16,0},{32,48},{48,32},{64,80},{80,64},{96,112},{112,96},{1... | collective-permute-start | bytes 196616 | tf_op jit(solution)/shard_map/ppermute | solution.py:386
